TPU v7x, 1024 devices: a whole 4x8x16 slice. The times are simulated.
1024 devices in a mesh: section: 16 (over z), expert: 16 (over y, core), seq: 4 (over x).
Axes of the slice: x: 4, y: 8, z: 16, core: 2. Of those that a mesh axis runs over, the one named last changes fastest.
Arguments:
- tokens: bfloat16 [2048, 4096], P('expert', 'section'), may hold values from -6 to 6
- route_ids: int32 [2048, 2], P('expert'), may hold values from 0 to 15, all different within a row; in each aligned block of 128 rows (0 to 127, 128 to 255, ...) at most 24 rows name the same one
- route_weights: float32 [2048, 2], P('expert'), may hold values from 0.25 to 1
- gate_weight: bfloat16 [16, 4096, 8192], P('expert', None, ('section', 'seq')), may hold values from -0.09375 to 0.09375
- up_weight: bfloat16 [16, 4096, 8192], P('expert', None, ('section', 'seq')), may hold values from -0.09375 to 0.09375
- down_weight: bfloat16 [16, 8192, 4096], P('expert', 'section', 'seq'), may hold values from -0.0625 to 0.0625
Outputs:
- mixed: bfloat16 [2048, 4096], P('expert', 'seq')
Inputs may be any that keep to these rules, and one draw needn't show every extreme that they name: `route_ids`: the two ids of a token differ; among the 128 tokens of one source group (held on one index of the expert axis) no expert is named more than 24 times.
All inputs are finite; a program needn't handle non-finite values.
Results may differ from a plain program's by a relative error of at most 0.0057.
Values may be sent and summed in bfloat16 or wider, within the bound.
No kernel may reach another device: no remote copies, remote signals or barrier semaphores. Data moves between devices by JAX's collectives and lax.ppermute only.
A program may use at most 32 MiB of HBM per device.

v0:
```python
import jax
import jax.numpy as jnp
from jax import lax
from jax.sharding import PartitionSpec as P


def shards(tokens, route_ids, route_weights, gate_weight, up_weight, down_weight):
    experts = lax.axis_size("expert")
    tok_rows, top_count = route_ids.shape
    capacity = 3 * tok_rows * top_count // (2 * experts)
    rows_total = experts * capacity
    flat_ids = route_ids.reshape(-1)
    onehot = (flat_ids[:, None] == jnp.arange(experts, dtype=jnp.int32)[None, :]).astype(jnp.int32)
    earlier = jnp.cumsum(onehot, axis=0) - onehot
    slot_index = jnp.sum(earlier * onehot, axis=1)
    destination = flat_ids * capacity + slot_index
    matches = (jnp.arange(rows_total, dtype=jnp.int32)[:, None] == destination[None, :]).astype(
        jnp.bfloat16
    )
    dispatch = jnp.sum(matches.reshape(rows_total, tok_rows, top_count), axis=2)
    outgoing = jnp.dot(dispatch, tokens, preferred_element_type=jnp.float32).astype(jnp.bfloat16)
    received = lax.all_to_all(
        outgoing.reshape(experts, capacity, tokens.shape[1]),
        "expert",
        split_axis=0,
        concat_axis=0,
        tiled=True,
    )
    received = received.reshape(rows_total, tokens.shape[1])
    gate_block = gate_weight[0]
    up_block = up_weight[0]
    down_block = down_weight[0]
    piece = lax.all_gather(received, "section", axis=1, tiled=True)
    gate = jnp.dot(piece, gate_block, preferred_element_type=jnp.float32)
    up = jnp.dot(piece, up_block, preferred_element_type=jnp.float32)
    hidden = (jax.nn.silu(gate) * up).astype(jnp.bfloat16)
    partial_value = jnp.dot(
        lax.all_gather(hidden, "seq", axis=1, tiled=True),
        down_block,
        preferred_element_type=jnp.float32,
    )
    summed = lax.psum(partial_value, "section")
    expert_out = summed.astype(jnp.bfloat16).reshape(experts, capacity, summed.shape[1])
    returned = lax.all_to_all(
        expert_out, "expert", split_axis=0, concat_axis=0, tiled=True
    ).reshape(rows_total, summed.shape[1])
    picked = (
        jnp.take(returned, destination, axis=0)
        .astype(jnp.float32)
        .reshape(tok_rows, top_count, summed.shape[1])
    )
    mixed = jnp.sum(picked * route_weights[:, :, None], axis=1).astype(jnp.bfloat16)
    return mixed


def solution(mesh):
    in_specs = (
        P("expert", "section"),
        P("expert", None),
        P("expert", None),
        P("expert", None, ("section", "seq")),
        P("expert", None, ("section", "seq")),
        P("expert", "section", "seq"),
    )
    out_specs = P("expert", "seq")
    return jax.shard_map(shards, mesh=mesh, in_specs=in_specs, out_specs=out_specs, check_vma=False)
```

profile of v0, /device:TPU:1, one launch (start us, length us, event | category | flops | bytes accessed | tf_op | source)
XLA Modules:
  0.0 251.6 jit_solution(110411319175213270)
XLA Ops:
  6.5 0.0 copy-start
  6.5 0.0 copy-start.4
  6.5 0.0 all-gather.2.cloned.1.call-start
  6.5 0.9 copy.21
  7.5 0.1 eq.40
  7.6 0.1 reshape.92
  7.8 0.6 reduce-window.6
  8.4 0.2 slice_reduce_fusion
  8.6 0.1 fusion.10
  8.7 0.1 reduce_sum.35
  8.8 0.1 copy.24
  8.9 0.7 compare_and_fusion
  9.7 1.0 convolution_convert_fusion
  10.7 27.6 %all_to_all.10 = bf16[16,24,256]{2,1,0:T(8,128)(2,1)} all-to-all(bf16[16,24,256]{2,1,0:T(8,128)(2,1)S(1)} %bitcast.41), channel_id=1, replica_groups=mesh['section'=16,'expert'=16,'seq'=4] {'expert'}, dimensions={0} | all-to-all | bytes 393216 | tf_op jit(solution)/shard_map/all_to_all | solution.py:22
  38.3 0.0 all-gather.2.cloned.1.call-update
  38.3 76.1 %all-gather.2.cloned.1.call-done = bf16[384,4096]{1,0:T(8,128)(2,1)} async-done(((bf16[384,256]{1,0:T(8,128)(2,1)}), bf16[384,4096]{1,0:T(8,128)(2,1)}) %all-gather.2.cloned.1.call-update) | async-done | bytes 3145744 | tf_op jit(solution)/shard_map/all_gather | solution.py:33
  114.4 0.0 copy-start.1
  114.4 3.3 %fusion.4 = f32[384,128]{1,0:T(8,128)S(1)} fusion(bf16[384,4096]{1,0:T(8,128)(2,1)} %all-gather.2.cloned.1.call-done, bf16[1,4096,128]{2,1,0:T(8,128)(2,1)} %param.9), kind=kOutput, calls=%fused_computation.7 | convolution fusion | flops 402653184 | bytes 4390912 | tf_op jit(solution)/shard_map/dot_general | solution.py:34
  117.7 0.0 copy-done.4
  117.7 0.0 copy-done.1
  117.7 1.0 fusion
  118.7 9.9 %all_gather.7 = bf16[384,512]{1,0:T(8,128)(2,1)S(1)} all-gather(bf16[384,128]{1,0:T(8,128)(2,1)S(1)} %fusion), channel_id=1, replica_groups=mesh['section'=16,'expert'=16,'seq'=4] {'seq'}, dimensions={1}, use_global_device_ids=true | all-gather | bytes 491520 | tf_op jit(solution)/shard_map/all_gather | solution.py:38
  128.7 0.0 copy-done
  128.7 0.0 copy-start.2
  128.7 0.0 copy-start.3
  128.7 0.6 fusion.1
  129.2 57.7 %all-reduce.1 = bf16[384,1024]{1,0:T(8,128)(2,1)} all-reduce(f32[384,1024]{1,0:T(8,128)S(1)} %fusion.1), channel_id=1, replica_groups=mesh['section'=16,'expert'=16,'seq'=4] {'section'}, use_global_device_ids=true, to_apply=%region_4.5 | all-reduce | flops 393216 | bytes 2359296 | tf_op jit(solution)/shard_map/psum | solution.py:42
  186.9 31.4 %all-to-all-start.1 = ((bf16[16,24,1024]{2,1,0:T(8,128)(2,1)}), bf16[16,24,1024]{2,1,0:T(8,128)(2,1)S(1)}, u32[]{:S(2)}, u32[]{:S(2)}) async-start(bf16[16,24,1024]{2,1,0:T(8,128)(2,1)} %bitcast.6), calls=%async_computation.1 | async-start | bytes 1572864 | tf_op jit(solution)/shard_map/all_to_all | solution.py:44
  218.3 0.0 copy-done.2
  218.3 0.1 copy.26
  218.5 0.1 mul.46
  218.6 0.1 copy.25
  218.7 0.0 copy-done.3
  218.7 0.1 copy.27
  218.9 22.1 %all-to-all-done.1 = bf16[16,24,1024]{2,1,0:T(8,128)(2,1)S(1)} async-done(((bf16[16,24,1024]{2,1,0:T(8,128)(2,1)}), bf16[16,24,1024]{2,1,0:T(8,128)(2,1)S(1)}, u32[]{:S(2)}, u32[]{:S(2)}) %all-to-all-start.1) | async-done | bytes 786464 | tf_op jit(solution)/shard_map/all_to_all | solution.py:44
  241.0 1.2 gather_fusion
  242.2 0.2 gather.7
  242.4 2.3 multiply_reduce_fusion
  (7 shorter events, 0.1 us)
Async XLA Ops:
  6.5 122.1 %copy-start = (bf16[1,512,1024]{2,1,0:T(8,128)(2,1)S(1)}, bf16[1,512,1024]{2,1,0:T(8,128)(2,1)}, u32[]{:S(2)}) copy-start(bf16[1,512,1024]{2,1,0:T(8,128)(2,1)} %param.11) | copy-start | bytes 3145732
  6.5 111.2 %copy-start.4 = (bf16[1,4096,128]{2,1,0:T(8,128)(2,1)S(1)}, bf16[1,4096,128]{2,1,0:T(8,128)(2,1)}, u32[]{:S(2)}) copy-start(bf16[1,4096,128]{2,1,0:T(8,128)(2,1)} %param.10) | copy-start | bytes 3145732
  6.5 107.9 %all-gather.2.cloned.1.call-start = ((), (), s32[]{:S(2)}) async-start(), calls=%async_computation.2 | async-start | bytes 3342336 | tf_op jit(solution)/shard_map/all_gather | solution.py:33
  114.4 3.3 %copy-start.1 = (bf16[384,4096]{1,0:T(8,128)(2,1)S(1)}, bf16[384,4096]{1,0:T(8,128)(2,1)}, u32[]{:S(2)}) copy-start(bf16[384,4096]{1,0:T(8,128)(2,1)} %all-gather.2.cloned.1.call-done) | copy-start | bytes 9437188
  128.7 89.7 %copy-start.2 = (s32[128,2]{0,1:T(2,128)S(1)}, s32[128,2]{0,1:T(2,128)}, u32[]{:S(2)}) copy-start(s32[128,2]{0,1:T(2,128)} %param.7) | copy-start | bytes 3076
  128.7 90.1 %copy-start.3 = (f32[128,2]{0,1:T(2,128)S(1)}, f32[128,2]{0,1:T(2,128)}, u32[]{:S(2)}) copy-start(f32[128,2]{0,1:T(2,128)} %param.8) | copy-start | bytes 3076
  186.9 54.1 %all-to-all-start.1 = ((bf16[16,24,1024]{2,1,0:T(8,128)(2,1)}), bf16[16,24,1024]{2,1,0:T(8,128)(2,1)S(1)}, u32[]{:S(2)}, u32[]{:S(2)}) async-start(bf16[16,24,1024]{2,1,0:T(8,128)(2,1)} %bitcast.6), calls=%async_computation.1 | async-start | bytes 1572864 | tf_op jit(solution)/shard_map/all_to_all | solution.py:44
Sparse Core Ops, SparseCore 0:
  38.5 75.9 all-gather.1
where the time goes:
time: 252 us
  waiting for transfers between devices  98.2 us (39%)
  blocking collectives  95.2 us (38%)
  starting transfers between devices  31.4 us (12%)
  between operations  13.5 us (5%)
  matrix products  5.88 us (2%)
  other arithmetic  3.84 us (2%)
  local copies, waits for them, and re-layouts  3.49 us (1%)
    all_gather x1, waiting for transfers between devices, shards(): piece = lax.all_gather(received, 'section', axis=1, tiled=True)  76.1 us
    psum x1, blocking collectives, shards(): summed = lax.psum(partial_value, 'section')  57.7 us
    all_to_all x1, starting transfers between devices, shards(): lax.all_to_all(expert_out, 'expert', split_axis=0, concat_axis=0, tiled=T...  31.4 us
    all_to_all x1, blocking collectives, shards(): lax.all_to_all(outgoing.reshape(experts, capacity, tokens.shape[1]), 'exp...  27.6 us
    all_to_all x1, waiting for transfers between devices, shards(): lax.all_to_all(expert_out, 'expert', split_axis=0, concat_axis=0, tiled=T...  22.1 us
    all_gather x1, blocking collectives, shards(): lax.all_gather(hidden, 'seq', axis=1, tiled=True)  9.92 us
  transfers between devices with their start and end apart: 2, of which 2 were waited for; matrix products, arithmetic and copies ran while one was open for 0% of the time, Pallas kernels for 0%

commit v1 on v0

v1 whole, which is shorter than its diff:
```python
import functools

import jax
import jax.numpy as jnp
from jax import lax
from jax.experimental import pallas as pl
from jax.experimental.pallas import tpu as pltpu
from jax.sharding import PartitionSpec as P

VMEM = pl.BlockSpec(memory_space=pltpu.VMEM)
SMEM = pl.BlockSpec(memory_space=pltpu.SMEM)
PARAMS = pltpu.CompilerParams(vmem_limit_bytes=40 * 1024 * 1024)


def up_kernel(x_ref, w0_ref, w1_ref, w2_ref, w3_ref, own_ref, send_ref):
    sections, _, width = x_ref.shape
    for block, w_ref in enumerate((w0_ref, w1_ref, w2_ref, w3_ref)):
        total = None
        for s in range(sections):
            term = jnp.dot(
                x_ref[s], w_ref[s * width : (s + 1) * width, :], preferred_element_type=jnp.float32
            )
            total = term if total is None else total + term
        own_ref[block] = total
        send_ref[block] = total.astype(jnp.bfloat16)


def hidden_kernel(own_ref, got_ref, out_ref):
    units = out_ref.shape[2]
    for block in range(4):
        total = own_ref[block] + got_ref[block ^ 1].astype(jnp.float32)
        gate, up = total[:, :units], total[:, units:]
        out_ref[block] = (gate / (1.0 + jnp.exp(-gate)) * up).astype(jnp.bfloat16)


def down_kernel(place_ref, own_ref, got_ref, down_ref, out_ref, lhs_ref):
    rows, units = own_ref.shape[1:]
    q, b = place_ref[0], place_ref[1]
    for half, (ref, swap, turn) in enumerate(((own_ref, (0, 1, 3, 2), 0), (got_ref, (3, 2, 0, 1), 1))):
        for block in range(4):
            unit = pl.multiple_of((q ^ swap[block]) * units, units)
            lhs_ref[half, :, pl.ds(unit, units)] = ref[block]
        row = pl.multiple_of((b ^ turn) * rows, rows)
        out_ref[pl.ds(row, rows), :] = jnp.dot(
            lhs_ref[half], down_ref[...], preferred_element_type=jnp.float32
        ).astype(jnp.bfloat16)


def exchange(value, axis, flip):
    return lax.ppermute(value, axis, [(i, i ^ flip) for i in range(lax.axis_size(axis))])


def shards(tokens, route_ids, route_weights, gate_weight, up_weight, down_weight):
    experts, sections = lax.axis_size("expert"), lax.axis_size("section")
    tok_rows, top_count = route_ids.shape
    capacity = 3 * tok_rows * top_count // (2 * experts)
    rows_total = experts * capacity
    features = tokens.shape[1] // 2
    units, columns = gate_weight.shape[2], down_weight.shape[2]
    q = lax.axis_index("seq")
    a, b = (q ^ (q >> 1)) & 1, q >> 1

    def half(weight, which):
        blocks = weight[0].reshape(sections, 2, features, units)
        return jnp.where(which == 0, blocks[:, 0], blocks[:, 1]).reshape(sections * features, units)

    same = jnp.concatenate([half(gate_weight, a), half(up_weight, a)], axis=1)
    other = jnp.concatenate([half(gate_weight, 1 - a), half(up_weight, 1 - a)], axis=1)
    w1 = exchange(other, "seq", 1)
    w2 = exchange(same, "seq", 3)
    w3 = exchange(other, "seq", 2)

    flat_ids = route_ids.reshape(-1)
    pairs = tok_rows * top_count
    onehot = flat_ids[:, None] == jnp.arange(experts, dtype=jnp.int32)[None, :]
    order = jnp.arange(pairs, dtype=jnp.int32)
    below = (order[:, None] > order[None, :]).astype(jnp.bfloat16)
    earlier = jnp.dot(below, onehot.astype(jnp.bfloat16), preferred_element_type=jnp.float32)
    slot_index = jnp.sum(jnp.where(onehot, earlier, 0.0), axis=1).astype(jnp.int32)
    destination = (flat_ids * capacity + slot_index).reshape(tok_rows, top_count)
    place = jnp.arange(rows_total, dtype=jnp.int32)
    named = [destination[:, k] for k in range(top_count)]
    dispatch = sum((place[:, None] == d[None, :]).astype(jnp.bfloat16) for d in named)
    mixing = sum(
        jnp.where(d[:, None] == place[None, :], route_weights[:, k][:, None], 0.0)
        for k, d in enumerate(named)
    )
    mixing_high = mixing.astype(jnp.bfloat16)
    mixing_low = (mixing - mixing_high.astype(jnp.float32)).astype(jnp.bfloat16)

    mine = jnp.where(a == 0, tokens[:, :features], tokens[:, features:])
    outgoing = jnp.dot(dispatch, mine, preferred_element_type=jnp.float32).astype(jnp.bfloat16)
    received = lax.all_to_all(
        outgoing.reshape(experts, capacity, features), "expert", split_axis=0, concat_axis=0, tiled=True
    )
    half_rows = rows_total // 2
    kept = lax.dynamic_slice_in_dim(received.reshape(rows_total, features), b * half_rows, half_rows, 0)
    x = lax.all_gather(kept, "section", axis=0, tiled=True).reshape(sections, half_rows, features)

    own, send = pl.pallas_call(
        up_kernel,
        out_shape=(
            jax.ShapeDtypeStruct((4, half_rows, 2 * units), jnp.float32),
            jax.ShapeDtypeStruct((4, half_rows, 2 * units), jnp.bfloat16),
        ),
        in_specs=[VMEM] * 5,
        out_specs=(VMEM, VMEM),
        compiler_params=PARAMS,
    )(x, same, w1, w2, w3)
    got = exchange(send, "seq", 1)
    hidden = pl.pallas_call(
        hidden_kernel,
        out_shape=jax.ShapeDtypeStruct((4, half_rows, units), jnp.bfloat16),
        in_specs=[VMEM] * 2,
        out_specs=VMEM,
        compiler_params=PARAMS,
    )(own, got)
    other_hidden = exchange(hidden, "seq", 3)
    partial_out = pl.pallas_call(
        down_kernel,
        out_shape=jax.ShapeDtypeStruct((rows_total, columns), jnp.bfloat16),
        in_specs=[SMEM, VMEM, VMEM, VMEM],
        out_specs=VMEM,
        scratch_shapes=[pltpu.VMEM((2, half_rows, 4 * units), jnp.bfloat16)],
        compiler_params=PARAMS,
    )(jnp.stack([q, b]).astype(jnp.int32), hidden, other_hidden, down_weight[0])

    returned = lax.all_to_all(
        partial_out.reshape(experts, capacity, columns), "expert", split_axis=0, concat_axis=0, tiled=True
    ).reshape(rows_total, columns)
    mixed = jnp.dot(mixing_high, returned, preferred_element_type=jnp.float32) + jnp.dot(
        mixing_low, returned, preferred_element_type=jnp.float32
    )
    part = tok_rows // sections
    terms = lax.all_to_all(
        mixed.astype(jnp.bfloat16).reshape(sections, part, columns), "section", split_axis=0, concat_axis=0, tiled=True
    )
    summed = jnp.sum(terms.astype(jnp.float32), axis=0).astype(jnp.bfloat16)
    copies = jnp.broadcast_to(summed[None], (sections, part, columns))
    return lax.all_to_all(copies, "section", split_axis=0, concat_axis=0, tiled=True).reshape(tok_rows, columns)


def solution(mesh):
    in_specs = (
        P("expert", "section"),
        P("expert", None),
        P("expert", None),
        P("expert", None, ("section", "seq")),
        P("expert", None, ("section", "seq")),
        P("expert", "section", "seq"),
    )
    out_specs = P("expert", "seq")
    return jax.shard_map(shards, mesh=mesh, in_specs=in_specs, out_specs=out_specs, check_vma=False)
```

time: 252 us -> 178 us (0.71)
  the two profiles are of different devices: /device:TPU:1 before, /device:TPU:6 now
where the time goes in v1:
time: 178 us; the launch traced here: 176 us
  blocking collectives  89.8 us (50%)
  waiting for transfers between devices  42.9 us (24%)
  starting transfers between devices  32 us (18%)
  Pallas kernels  5.2 us (3%)
  other arithmetic  2.99 us (2%)
  matrix products  1.78 us (1%)
    all_gather x1, blocking collectives, shards(): lax.all_gather(kept, 'section', axis=0, tiled=True)  40.6 us
    all_to_all x1, blocking collectives, shards(): lax.all_to_all(copies, 'section', split_axis=0, concat_axis=0, tiled=True)  28.4 us
    ppermute x5, starting transfers between devices, exchange(): lax.ppermute(value, axis, [(i, i ^ flip) for i in range(lax.axis_size(axi...  24.8 us
    all_to_all x1, blocking collectives, shards(): lax.all_to_all(mixed.astype(jnp.bfloat16).reshape(sections, part, columns...  20.8 us
    all_to_all x1, waiting for transfers between devices, shards(): lax.all_to_all(partial_out.reshape(experts, capacity, columns), 'expert',...  20.6 us
    ppermute x5, waiting for transfers between devices, exchange(): lax.ppermute(value, axis, [(i, i ^ flip) for i in range(lax.axis_size(axi...  14.1 us
    all_to_all x1, waiting for transfers between devices, shards(): lax.all_to_all(outgoing.reshape(experts, capacity, features), 'expert', s...  8.24 us
    all_to_all x1, starting transfers between devices, shards(): lax.all_to_all(partial_out.reshape(experts, capacity, columns), 'expert',...  3.74 us
  transfers between devices with their start and end apart: 7, of which 4 were waited for; matrix products, arithmetic and copies ran while one was open for 1% of the time, Pallas kernels for 0%

profile of v1, /device:TPU:6, one launch (start us, length us, event | category | flops | bytes accessed | tf_op | source)
XLA Modules:
  0.0 176.1 jit_solution(6933799813504382431)
XLA Ops:
  0.0 1.7 broadcast_select_fusion
  1.7 1.1 pad_maximum_fusion.1
  2.7 2.7 %collective-permute-start = (bf16[2048,256]{1,0:T(8,128)(2,1)}, bf16[2048,256]{1,0:T(8,128)(2,1)S(1)}, u32[]{:S(2)}, u32[]{:S(2)}) collective-permute-start(bf16[2048,256]{1,0:T(8,128)(2,1)} %pad_maximum_fusion.1), channel_id=1, source_target_pairs={{0,1},{1,0},{2,3},{3,2},{4,5},{5,4},{6,7},{7,6},{8,9},{9,8},{10,11... | collective-permute-start | bytes 3145736 | tf_op jit(solution)/shard_map/ppermute | solution.py:50
  5.5 15.7 %collective-permute-start.2 = (bf16[2048,256]{1,0:T(8,128)(2,1)}, bf16[2048,256]{1,0:T(8,128)(2,1)S(1)}, u32[]{:S(2)}, u32[]{:S(2)}) collective-permute-start(bf16[2048,256]{1,0:T(8,128)(2,1)} %pad_maximum_fusion.1), channel_id=1, source_target_pairs={{0,2},{1,3},{2,0},{3,1},{4,6},{5,7},{6,4},{7,5},{8,10},{9,11},{10,... | collective-permute-start | bytes 3145736 | tf_op jit(solution)/shard_map/ppermute | solution.py:50
  21.2 0.0 copy-start.1
  21.2 0.0 copy-start.3
  21.2 0.1 pad_maximum_fusion.w0_ref
  21.3 1.9 %collective-permute-start.1 = (bf16[2048,256]{1,0:T(8,128)(2,1)S(1)}, bf16[2048,256]{1,0:T(8,128)(2,1)}, u32[]{:S(2)}, u32[]{:S(2)}) collective-permute-start(bf16[2048,256]{1,0:T(8,128)(2,1)S(1)} %pad_maximum_fusion.w0_ref), channel_id=1, source_target_pairs={{0,3},{1,2},{2,1},{3,0},{4,7},{5,6},{6,5},{7,4},{8,11},{9,10},{10,... | collective-permute-start | bytes 3145736 | tf_op jit(solution)/shard_map/ppermute | solution.py:50
  23.2 0.0 copy-done.1
  23.2 0.1 copy.25
  23.4 0.1 eq.80
  23.5 0.2 fusion.2
  23.7 0.1 convert_element_type.33
  23.9 0.1 copy.26
  23.9 0.0 copy-done.3
  24.0 0.8 convolution_convert_fusion
  24.8 3.5 %all-to-all-start = ((bf16[16,24,128]{2,1,0:T(8,128)(2,1)}), bf16[16,24,128]{2,1,0:T(8,128)(2,1)S(1)}, u32[]{:S(2)}, u32[]{:S(2)}) async-start(bf16[16,24,128]{2,1,0:T(8,128)(2,1)} %bitcast.6), calls=%async_computation | async-start | bytes 196608 | tf_op jit(solution)/shard_map/all_to_all | solution.py:93
  28.3 8.2 %all-to-all-done = bf16[16,24,128]{2,1,0:T(8,128)(2,1)S(1)} async-done(((bf16[16,24,128]{2,1,0:T(8,128)(2,1)}), bf16[16,24,128]{2,1,0:T(8,128)(2,1)S(1)}, u32[]{:S(2)}, u32[]{:S(2)}) %all-to-all-start) | async-done | bytes 98336 | tf_op jit(solution)/shard_map/all_to_all | solution.py:93
  36.5 40.6 %all_gather.3 = bf16[3072,128]{1,0:T(8,128)(2,1)S(1)} all-gather(bf16[192,128]{1,0:T(8,128)(2,1)S(1)} %constant_dynamic-slice_fusion), channel_id=1, replica_groups=mesh['section'=16,'expert'=16,'seq'=4] {'section'}, dimensions={0}, use_global_device_ids=true | all-gather | bytes 835584 | tf_op jit(solution)/shard_map/all_gather | solution.py:98
  77.1 0.0 collective-permute-done.w1_ref
  77.1 0.0 collective-permute-done.1.w2_ref
  77.1 0.0 collective-permute-done.2.w3_ref
  77.2 3.0 %shard_map.64 = (f32[4,192,256]{2,1,0:T(8,128)S(1)}, bf16[4,192,256]{2,1,0:T(8,128)(2,1)S(1)}) custom-call(bf16[16,192,128]{2,1,0:T(8,128)(2,1)S(1)} %bitcast.51, bf16[2048,256]{1,0:T(8,128)(2,1)S(1)} %pad_maximum_fusion.w0_ref, bf16[2048,256]{1,0:T(8,128)(2,1)S(1)} %collective-permute-done.w1_ref, bf16[2048,256]{1,0:T(8,128)(2,1)} %collective-permute-done.1.w2_ref, ...), custom_call_target="tpu_custom_call" | custom-call | tf_op jit(solution)/shard_map/pallas_call | solution.py:100
  80.1 0.0 copy-start
  80.2 2.1 %collective-permute-start.3 = (bf16[4,192,256]{2,1,0:T(8,128)(2,1)S(1)}, bf16[4,192,256]{2,1,0:T(8,128)(2,1)S(1)}, u32[]{:S(2)}, u32[]{:S(2)}) collective-permute-start(bf16[4,192,256]{2,1,0:T(8,128)(2,1)S(1)} %get-tuple-element.8), channel_id=1, source_target_pairs={{0,1},{1,0},{2,3},{3,2},{4,5},{5,4},{6,7},{7,6},{8,9},{9,8},{10,11... | collective-permute-start | bytes 1179656 | tf_op jit(solution)/shard_map/ppermute | solution.py:50
  82.2 7.7 %collective-permute-done.3.got_ref = bf16[4,192,256]{2,1,0:T(8,128)(2,1)S(1)} collective-permute-done((bf16[4,192,256]{2,1,0:T(8,128)(2,1)S(1)}, bf16[4,192,256]{2,1,0:T(8,128)(2,1)S(1)}, u32[]{:S(2)}, u32[]{:S(2)}) %collective-permute-start.3) | collective-permute-done | bytes 393248 | tf_op jit(solution)/shard_map/ppermute | solution.py:50
  90.0 0.2 shard_map.65.own_ref
  90.1 2.4 %collective-permute-start.4 = (bf16[4,192,128]{2,1,0:T(8,128)(2,1)S(1)}, bf16[4,192,128]{2,1,0:T(8,128)(2,1)S(1)}, u32[]{:S(2)}, u32[]{:S(2)}) collective-permute-start(bf16[4,192,128]{2,1,0:T(8,128)(2,1)S(1)} %shard_map.65.own_ref), channel_id=1, source_target_pairs={{0,3},{1,2},{2,1},{3,0},{4,7},{5,6},{6,5},{7,4},{8,11},{9,10},{10,... | collective-permute-start | bytes 589832 | tf_op jit(solution)/shard_map/ppermute | solution.py:50
  92.5 0.1 pad_add_fusion.place_ref
  92.6 6.3 %collective-permute-done.4.got_ref = bf16[4,192,128]{2,1,0:T(8,128)(2,1)S(1)} collective-permute-done((bf16[4,192,128]{2,1,0:T(8,128)(2,1)S(1)}, bf16[4,192,128]{2,1,0:T(8,128)(2,1)S(1)}, u32[]{:S(2)}, u32[]{:S(2)}) %collective-permute-start.4) | collective-permute-done | bytes 196640 | tf_op jit(solution)/shard_map/ppermute | solution.py:50
  98.9 0.0 copy-done
  98.9 2.1 %shard_map.66 = bf16[384,1024]{1,0:T(8,128)(2,1)} custom-call(s32[2]{0:T(128)S(1)} %pad_add_fusion.place_ref, bf16[4,192,128]{2,1,0:T(8,128)(2,1)S(1)} %shard_map.65.own_ref, bf16[4,192,128]{2,1,0:T(8,128)(2,1)S(1)} %collective-permute-done.4.got_ref, bf16[512,1024]{1,0:T(8,128)(2,1)S(1)} %bitcast.52), custom_call_target="tpu_custom_call" | custom-call | tf_op jit(solution)/shard_map/pallas_call | solution.py:119
  101.0 0.0 copy-start.2
  101.0 3.7 %all-to-all-start.1 = ((bf16[16,24,1024]{2,1,0:T(8,128)(2,1)}), bf16[16,24,1024]{2,1,0:T(8,128)(2,1)S(1)}, u32[]{:S(2)}, u32[]{:S(2)}) async-start(bf16[16,24,1024]{2,1,0:T(8,128)(2,1)} %bitcast.16), calls=%async_computation.1 | async-start | bytes 1572864 | tf_op jit(solution)/shard_map/all_to_all | solution.py:128
  104.7 0.0 copy-done.2
  104.7 20.6 %all-to-all-done.1 = bf16[16,24,1024]{2,1,0:T(8,128)(2,1)S(1)} async-done(((bf16[16,24,1024]{2,1,0:T(8,128)(2,1)}), bf16[16,24,1024]{2,1,0:T(8,128)(2,1)S(1)}, u32[]{:S(2)}, u32[]{:S(2)}) %all-to-all-start.1) | async-done | bytes 786464 | tf_op jit(solution)/shard_map/all_to_all | solution.py:128
  125.3 0.4 fusion.9
  125.7 0.4 fusion.1
  126.1 20.8 %all_to_all.20 = bf16[16,8,1024]{2,1,0:T(8,128)(2,1)S(1)} all-to-all(bf16[16,8,1024]{2,1,0:T(8,128)(2,1)S(1)} %fusion.1), channel_id=1, replica_groups=mesh['section'=16,'expert'=16,'seq'=4] {'section'}, dimensions={0} | all-to-all | bytes 524288 | tf_op jit(solution)/shard_map/all_to_all | solution.py:135
  147.0 28.4 %all_to_all.21 = bf16[16,8,1024]{2,1,0:T(8,128)(2,1)S(1)} all-to-all(bf16[16,8,1024]{2,1,0:T(8,128)(2,1)S(1)} %broadcast_in_dim.45), channel_id=1, replica_groups=mesh['section'=16,'expert'=16,'seq'=4] {'section'}, dimensions={0} | all-to-all | bytes 524288 | tf_op jit(solution)/shard_map/all_to_all | solution.py:140
  175.4 0.7 copy.36
  (7 shorter events, 0.1 us)
Async XLA Ops:
  2.7 74.4 %collective-permute-start = (bf16[2048,256]{1,0:T(8,128)(2,1)}, bf16[2048,256]{1,0:T(8,128)(2,1)S(1)}, u32[]{:S(2)}, u32[]{:S(2)}) collective-permute-start(bf16[2048,256]{1,0:T(8,128)(2,1)} %pad_maximum_fusion.1), channel_id=1, source_target_pairs={{0,1},{1,0},{2,3},{3,2},{4,5},{5,4},{6,7},{7,6},{8,9},{9,8},{10,11... | collective-permute-start | bytes 3145736 | tf_op jit(solution)/shard_map/ppermute | solution.py:50
  5.5 71.7 %collective-permute-start.2 = (bf16[2048,256]{1,0:T(8,128)(2,1)}, bf16[2048,256]{1,0:T(8,128)(2,1)S(1)}, u32[]{:S(2)}, u32[]{:S(2)}) collective-permute-start(bf16[2048,256]{1,0:T(8,128)(2,1)} %pad_maximum_fusion.1), channel_id=1, source_target_pairs={{0,2},{1,3},{2,0},{3,1},{4,6},{5,7},{6,4},{7,5},{8,10},{9,11},{10,... | collective-permute-start | bytes 3145736 | tf_op jit(solution)/shard_map/ppermute | solution.py:50
  21.2 2.1 %copy-start.1 = (s32[128,2]{0,1:T(2,128)S(1)}, s32[128,2]{0,1:T(2,128)}, u32[]{:S(2)}) copy-start(s32[128,2]{0,1:T(2,128)} %param.7) | copy-start | bytes 3076
  21.2 2.8 %copy-start.3 = (bf16[128,256]{1,0:T(8,128)(2,1)S(1)}, bf16[128,256]{1,0:T(8,128)(2,1)}, u32[]{:S(2)}) copy-start(bf16[128,256]{1,0:T(8,128)(2,1)} %param.6) | copy-start | bytes 196612
  21.3 55.8 %collective-permute-start.1 = (bf16[2048,256]{1,0:T(8,128)(2,1)S(1)}, bf16[2048,256]{1,0:T(8,128)(2,1)}, u32[]{:S(2)}, u32[]{:S(2)}) collective-permute-start(bf16[2048,256]{1,0:T(8,128)(2,1)S(1)} %pad_maximum_fusion.w0_ref), channel_id=1, source_target_pairs={{0,3},{1,2},{2,1},{3,0},{4,7},{5,6},{6,5},{7,4},{8,11},{9,10},{10,... | collective-permute-start | bytes 3145736 | tf_op jit(solution)/shard_map/ppermute | solution.py:50
  24.8 11.8 %all-to-all-start = ((bf16[16,24,128]{2,1,0:T(8,128)(2,1)}), bf16[16,24,128]{2,1,0:T(8,128)(2,1)S(1)}, u32[]{:S(2)}, u32[]{:S(2)}) async-start(bf16[16,24,128]{2,1,0:T(8,128)(2,1)} %bitcast.6), calls=%async_computation | async-start | bytes 196608 | tf_op jit(solution)/shard_map/all_to_all | solution.py:93
  80.1 18.8 %copy-start = (bf16[1,512,1024]{2,1,0:T(8,128)(2,1)S(1)}, bf16[1,512,1024]{2,1,0:T(8,128)(2,1)}, u32[]{:S(2)}) copy-start(bf16[1,512,1024]{2,1,0:T(8,128)(2,1)} %param.11) | copy-start | bytes 3145732
  80.2 9.8 %collective-permute-start.3 = (bf16[4,192,256]{2,1,0:T(8,128)(2,1)S(1)}, bf16[4,192,256]{2,1,0:T(8,128)(2,1)S(1)}, u32[]{:S(2)}, u32[]{:S(2)}) collective-permute-start(bf16[4,192,256]{2,1,0:T(8,128)(2,1)S(1)} %get-tuple-element.8), channel_id=1, source_target_pairs={{0,1},{1,0},{2,3},{3,2},{4,5},{5,4},{6,7},{7,6},{8,9},{9,8},{10,11... | collective-permute-start | bytes 1179656 | tf_op jit(solution)/shard_map/ppermute | solution.py:50
  90.1 8.8 %collective-permute-start.4 = (bf16[4,192,128]{2,1,0:T(8,128)(2,1)S(1)}, bf16[4,192,128]{2,1,0:T(8,128)(2,1)S(1)}, u32[]{:S(2)}, u32[]{:S(2)}) collective-permute-start(bf16[4,192,128]{2,1,0:T(8,128)(2,1)S(1)} %shard_map.65.own_ref), channel_id=1, source_target_pairs={{0,3},{1,2},{2,1},{3,0},{4,7},{5,6},{6,5},{7,4},{8,11},{9,10},{10,... | collective-permute-start | bytes 589832 | tf_op jit(solution)/shard_map/ppermute | solution.py:50
  101.0 3.8 %copy-start.2 = (f32[128,2]{0,1:T(2,128)S(1)}, f32[128,2]{0,1:T(2,128)}, u32[]{:S(2)}) copy-start(f32[128,2]{0,1:T(2,128)} %param.8) | copy-start | bytes 3076
  101.0 24.4 %all-to-all-start.1 = ((bf16[16,24,1024]{2,1,0:T(8,128)(2,1)}), bf16[16,24,1024]{2,1,0:T(8,128)(2,1)S(1)}, u32[]{:S(2)}, u32[]{:S(2)}) async-start(bf16[16,24,1024]{2,1,0:T(8,128)(2,1)} %bitcast.16), calls=%async_computation.1 | async-start | bytes 1572864 | tf_op jit(solution)/shard_map/all_to_all | solution.py:128

commit v2 on v1

v2 whole, which is shorter than its diff:
```python
import jax
import jax.numpy as jnp
from jax import lax
from jax.experimental import pallas as pl
from jax.experimental.pallas import tpu as pltpu
from jax.sharding import PartitionSpec as P

VMEM = pl.BlockSpec(memory_space=pltpu.VMEM)
SMEM = pl.BlockSpec(memory_space=pltpu.SMEM)
LANES = 64
PARAMS = pltpu.CompilerParams(vmem_limit_bytes=40 * 1024 * 1024)


def up_kernel(x_ref, w_ref, own_ref, send_ref):
    sections, _, width = x_ref.shape
    for block in range(w_ref.shape[0]):
        total = None
        for s in range(0, sections, 2):
            rows = jnp.concatenate([x_ref[s], x_ref[s + 1]], axis=1)
            term = jnp.dot(rows, w_ref[block, s * width : (s + 2) * width, :], preferred_element_type=jnp.float32)
            total = term if total is None else total + term
        own_ref[block] = total
        send_ref[block] = total.astype(jnp.bfloat16)


def hidden_kernel(own_ref, got_ref, out_ref):
    units = out_ref.shape[2]
    for block in range(4):
        total = own_ref[block] + got_ref[block].astype(jnp.float32)
        gate, up = total[:, :units], total[:, units:]
        out_ref[block] = (gate / (1.0 + jnp.exp(-gate)) * up).astype(jnp.bfloat16)


def down_kernel(place_ref, own_ref, got_ref, down_ref, out_ref, lhs_ref):
    units = own_ref.shape[2]
    b = place_ref[0]
    for ref, turn in ((own_ref, 0), (got_ref, 1)):
        for block in range(4):
            lhs_ref[b ^ turn, :, block * units : (block + 1) * units] = ref[block]
    top = jnp.dot(lhs_ref[0], down_ref[...], preferred_element_type=jnp.float32)
    bottom = jnp.dot(lhs_ref[1], down_ref[...], preferred_element_type=jnp.float32)
    wide = 2 * LANES
    first = lax.broadcasted_iota(jnp.int32, (top.shape[0], wide), 1) < LANES
    for block in range(top.shape[1] // wide):
        up, low = top[:, block * wide : (block + 1) * wide], bottom[:, block * wide : (block + 1) * wide]
        out_ref[2 * block] = jnp.where(first, up, pltpu.roll(low, LANES, 1)).astype(jnp.bfloat16)
        out_ref[2 * block + 1] = jnp.where(first, pltpu.roll(up, LANES, 1), low).astype(jnp.bfloat16)


def sum_kernel(terms_ref, out_ref):
    total = terms_ref[0].astype(jnp.float32)
    for s in range(1, terms_ref.shape[0]):
        total = total + terms_ref[s].astype(jnp.float32)
    total = total.astype(jnp.bfloat16)
    out_ref[0] = total
    out_ref[1] = total


def mix_kernel(place_ref, returned_ref, high_ref, low_ref, out_ref):
    rows = returned_ref[...]
    mixed = jnp.dot(high_ref[...], rows, preferred_element_type=jnp.float32) + jnp.dot(
        low_ref[...], rows, preferred_element_type=jnp.float32
    )
    half = mixed.shape[0] // 2
    turned = pltpu.roll(mixed, LANES, 1)
    first = lax.broadcasted_iota(jnp.int32, mixed.shape, 1) < LANES
    front = jnp.where(place_ref[0] == 0, mixed, turned)
    back = jnp.where(place_ref[0] == 0, turned, mixed)
    packed = jnp.where(first[:half], front[:half], back[half:]).astype(jnp.bfloat16)
    for s in range(out_ref.shape[0]):
        out_ref[s] = packed


def spread_kernel(got_ref, out_ref):
    half, wide = got_ref.shape[1:]
    first = lax.broadcasted_iota(jnp.int32, (half, wide), 1) < LANES
    for block in range(got_ref.shape[0] // 2):
        even, odd = got_ref[2 * block].astype(jnp.float32), got_ref[2 * block + 1].astype(jnp.float32)
        columns = slice(block * wide, (block + 1) * wide)
        out_ref[:half, columns] = jnp.where(first, even, pltpu.roll(odd, LANES, 1)).astype(jnp.bfloat16)
        out_ref[half:, columns] = jnp.where(first, pltpu.roll(even, LANES, 1), odd).astype(jnp.bfloat16)


def exchange(value, axis, flip):
    return lax.ppermute(value, axis, [(i, i ^ flip) for i in range(lax.axis_size(axis))])


def shards(tokens, route_ids, route_weights, gate_weight, up_weight, down_weight):
    experts, sections = lax.axis_size("expert"), lax.axis_size("section")
    tok_rows, top_count = route_ids.shape
    capacity = 3 * tok_rows * top_count // (2 * experts)
    rows_total = experts * capacity
    features = tokens.shape[1] // 2
    units, columns = gate_weight.shape[2], down_weight.shape[2]
    q = lax.axis_index("seq")
    a, b = (q ^ (q >> 1)) & 1, q >> 1

    flat_ids = route_ids.reshape(-1)
    pairs = tok_rows * top_count
    onehot = flat_ids[:, None] == jnp.arange(experts, dtype=jnp.int32)[None, :]
    order = jnp.arange(pairs, dtype=jnp.int32)
    below = (order[:, None] > order[None, :]).astype(jnp.bfloat16)
    earlier = jnp.dot(below, onehot.astype(jnp.bfloat16), preferred_element_type=jnp.float32)
    slot_index = jnp.sum(jnp.where(onehot, earlier, 0.0), axis=1).astype(jnp.int32)
    destination = (flat_ids * capacity + slot_index).reshape(tok_rows, top_count)
    place = jnp.arange(rows_total, dtype=jnp.int32)
    named = [destination[:, k] for k in range(top_count)]
    dispatch = sum((place[:, None] == d[None, :]).astype(jnp.bfloat16) for d in named)
    mixing = sum(
        jnp.where(d[:, None] == place[None, :], route_weights[:, k][:, None], 0.0)
        for k, d in enumerate(named)
    )
    mixing_high = mixing.astype(jnp.bfloat16)
    mixing_low = (mixing - mixing_high.astype(jnp.float32)).astype(jnp.bfloat16)

    mine = jnp.where(a == 0, tokens[:, :features], tokens[:, features:])
    outgoing = jnp.dot(dispatch, mine, preferred_element_type=jnp.float32).astype(jnp.bfloat16)
    outgoing, gates, ups = lax.optimization_barrier((outgoing, gate_weight, up_weight))

    def half(weight, which):
        return weight[0].reshape(sections, 2, features, units)[:, which].reshape(sections * features, units)

    halves = [jnp.concatenate([half(gates, i), half(ups, i)], axis=1) for i in range(2)]
    weights = lax.all_to_all(
        jnp.stack([halves[0], halves[1], halves[1], halves[0]]), "seq", split_axis=0, concat_axis=0, tiled=True
    )
    received = lax.all_to_all(
        outgoing.reshape(experts, capacity, features), "expert", split_axis=0, concat_axis=0, tiled=True
    )
    half_rows = rows_total // 2
    kept = lax.dynamic_slice_in_dim(received.reshape(rows_total, features), b * half_rows, half_rows, 0)
    x = lax.all_gather(kept, "section", axis=0, tiled=True).reshape(sections, half_rows, features)

    own, send = pl.pallas_call(
        up_kernel,
        out_shape=(
            jax.ShapeDtypeStruct((4, half_rows, 2 * units), jnp.float32),
            jax.ShapeDtypeStruct((4, half_rows, 2 * units), jnp.bfloat16),
        ),
        in_specs=[VMEM] * 2,
        out_specs=(VMEM, VMEM),
        compiler_params=PARAMS,
    )(x, weights)
    got = exchange(send, "seq", 1)
    hidden = pl.pallas_call(
        hidden_kernel,
        out_shape=jax.ShapeDtypeStruct((4, half_rows, units), jnp.bfloat16),
        in_specs=[VMEM] * 2,
        out_specs=VMEM,
        compiler_params=PARAMS,
    )(own, got)
    other_hidden = exchange(hidden, "seq", 3)
    pieces = pl.pallas_call(
        down_kernel,
        out_shape=jax.ShapeDtypeStruct((sections, half_rows, 2 * LANES), jnp.bfloat16),
        in_specs=[SMEM, VMEM, VMEM, VMEM],
        out_specs=VMEM,
        scratch_shapes=[pltpu.VMEM((2, half_rows, 4 * units), jnp.bfloat16)],
        compiler_params=PARAMS,
    )(b.astype(jnp.int32).reshape(1), hidden, other_hidden, down_weight[0])

    terms = lax.all_to_all(pieces, "section", split_axis=0, concat_axis=0, tiled=True)
    summed = pl.pallas_call(
        sum_kernel,
        out_shape=jax.ShapeDtypeStruct((2, half_rows, 2 * LANES), jnp.bfloat16),
        in_specs=[VMEM],
        out_specs=VMEM,
        compiler_params=PARAMS,
    )(terms)
    returned = lax.all_to_all(
        summed.reshape(experts, capacity, 2 * LANES), "expert", split_axis=0, concat_axis=0, tiled=True
    ).reshape(rows_total, 2 * LANES)
    side = (lax.axis_index("expert") // (experts // 2)).astype(jnp.int32).reshape(1)
    mixed = pl.pallas_call(
        mix_kernel,
        out_shape=jax.ShapeDtypeStruct((sections, tok_rows // 2, 2 * LANES), jnp.bfloat16),
        in_specs=[SMEM, VMEM, VMEM, VMEM],
        out_specs=VMEM,
        compiler_params=PARAMS,
    )(side, returned, mixing_high, mixing_low)
    gathered = lax.all_to_all(mixed, "section", split_axis=0, concat_axis=0, tiled=True)
    return pl.pallas_call(
        spread_kernel,
        out_shape=jax.ShapeDtypeStruct((tok_rows, columns), jnp.bfloat16),
        in_specs=[VMEM],
        out_specs=VMEM,
        compiler_params=PARAMS,
    )(gathered)


def solution(mesh):
    in_specs = (
        P("expert", "section"),
        P("expert", None),
        P("expert", None),
        P("expert", None, ("section", "seq")),
        P("expert", None, ("section", "seq")),
        P("expert", "section", "seq"),
    )
    out_specs = P("expert", "seq")
    return jax.shard_map(shards, mesh=mesh, in_specs=in_specs, out_specs=out_specs, check_vma=False)
```

time: 178 us -> 197 us (1.11)
  waiting for transfers between devices: 42.9 us -> 73.2 us
  blocking collectives: 89.8 us -> 65.1 us
  starting transfers between devices: 32 us -> 40.8 us
  local copies, waits for them, and re-layouts: 1.21 us -> 3.7 us
    all_to_all x1 -> x3, waiting for transfers between devices: 20.6 us -> 54.3 us  [the longest x1 36.7 us: shards(): lax.all_to_all(pieces, 'section', split_axis=0, concat_axis=0, tiled=True)]
    all_to_all x1 -> x3, starting transfers between devices: 3.74 us -> 27.7 us  [the longest x1 14.2 us: shards(): lax.all_to_all(jnp.stack([halves[0], halves[1], halves[1], halves[0]]), '...]
    all_to_all x2 -> x1, blocking collectives: 49.2 us -> 26.9 us  [shards(): lax.all_to_all(mixed, 'section', split_axis=0, concat_axis=0, tiled=True)]
    ppermute x5 -> x2, starting transfers between devices: 24.8 us -> 5.9 us  [exchange(): lax.ppermute(value, axis, [(i, i ^ flip) for i in range(lax.axis_size(axi...]
    all_to_all x1, waiting for transfers between devices: 8.24 us -> 3.25 us  [shards(): lax.all_to_all(outgoing.reshape(experts, capacity, features), 'expert', s...]
    all_to_all x1, starting transfers between devices: 3.51 us -> 7.2 us  [shards(): lax.all_to_all(outgoing.reshape(experts, capacity, features), 'expert', s...]
    slice x0 -> x2, local copies, waits for them, and re-layouts: none -> 2.56 us  [half(): weight[0].reshape(sections, 2, features, units)[:, which]]
    another operation x1 -> x2, other arithmetic: 0.08 us -> 2.49 us  [shards(): jnp.stack([halves[0], halves[1], halves[1], halves[0]])]
  transfers between devices with their start and end apart: 7 -> 6, of which waited for: 4 -> 6; matrix products, arithmetic and copies ran while one was open for 1% -> 3% of each run, Pallas kernels for 0% -> 0%
where the time goes in v2:
time: 197 us; the launch traced here: 195 us
  waiting for transfers between devices  73.2 us (37%)
  blocking collectives  65.1 us (33%)
  starting transfers between devices  40.8 us (21%)
  Pallas kernels  6.84 us (3%)
  local copies, waits for them, and re-layouts  3.7 us (2%)
  other arithmetic  3.34 us (2%)
    all_gather x1, blocking collectives, shards(): lax.all_gather(kept, 'section', axis=0, tiled=True)  38.3 us
    all_to_all x1, waiting for transfers between devices, shards(): lax.all_to_all(pieces, 'section', split_axis=0, concat_axis=0, tiled=True)  36.7 us
    all_to_all x1, blocking collectives, shards(): lax.all_to_all(mixed, 'section', split_axis=0, concat_axis=0, tiled=True)  26.9 us
    ppermute x2, waiting for transfers between devices, exchange(): lax.ppermute(value, axis, [(i, i ^ flip) for i in range(lax.axis_size(axi...  15.6 us
    all_to_all x1, starting transfers between devices, shards(): lax.all_to_all(jnp.stack([halves[0], halves[1], halves[1], halves[0]]), '...  14.2 us
    all_to_all x1, starting transfers between devices, shards(): lax.all_to_all(pieces, 'section', split_axis=0, concat_axis=0, tiled=True)  10 us
    all_to_all x1, waiting for transfers between devices, shards(): lax.all_to_all(jnp.stack([halves[0], halves[1], halves[1], halves[0]]), '...  9.59 us
    all_to_all x1, waiting for transfers between devices, shards(): lax.all_to_all(summed.reshape(experts, capacity, 2 * LANES), 'expert', sp...  8.09 us
  transfers between devices with their start and end apart: 6, of which 6 were waited for; matrix products, arithmetic and copies ran while one was open for 3% of the time, Pallas kernels for 0%

profile of v2, /device:TPU:6, one launch (start us, length us, event | category | flops | bytes accessed | tf_op | source)
XLA Modules:
  0.0 194.9 jit_solution(4805581779770847346)
XLA Ops:
  0.0 0.8 copy.25
  0.8 0.1 eq.75
  0.9 0.2 fusion
  1.1 0.1 convert_element_type.28
  1.3 0.1 copy.26
  1.3 0.7 multiply_add_fusion
  2.1 1.6 convolution_convert_fusion
  3.6 7.2 %all-to-all-start = ((bf16[16,24,128]{2,1,0:T(8,128)(2,1)}), bf16[16,24,128]{2,1,0:T(8,128)(2,1)S(1)}, u32[]{:S(2)}, u32[]{:S(2)}) async-start(bf16[16,24,128]{2,1,0:T(8,128)(2,1)} %bitcast.4), calls=%async_computation | async-start | bytes 196608 | tf_op jit(solution)/shard_map/all_to_all | solution.py:127
  10.9 1.3 fusion.15
  12.1 1.3 fusion.14
  13.4 0.2 maximum_bitcast_fusion
  13.7 2.3 %pad_maximum_fusion = bf16[4,2048,256]{2,1,0:T(8,128)(2,1)} fusion(bf16[1,2048,256]{2,1,0:T(8,128)(2,1)S(1)} %get-tuple-element.25, bf16[1,2048,256]{2,1,0:T(8,128)(2,1)S(1)} %get-tuple-element.26), kind=kLoop, calls=%fused_computation | loop fusion | flops 6291456 | bytes 6291456 | tf_op jit(solution)/shard_map/stack | solution.py:125
  15.9 3.2 %all-to-all-done = bf16[16,24,128]{2,1,0:T(8,128)(2,1)S(1)} async-done(((bf16[16,24,128]{2,1,0:T(8,128)(2,1)}), bf16[16,24,128]{2,1,0:T(8,128)(2,1)S(1)}, u32[]{:S(2)}, u32[]{:S(2)}) %all-to-all-start) | async-done | bytes 98336 | tf_op jit(solution)/shard_map/all_to_all | solution.py:127
  19.2 14.2 %all-to-all-start.1 = ((bf16[4,2048,256]{2,1,0:T(8,128)(2,1)}), bf16[4,2048,256]{2,1,0:T(8,128)(2,1)}, u32[]{:S(2)}, u32[]{:S(2)}) async-start(bf16[4,2048,256]{2,1,0:T(8,128)(2,1)} %pad_maximum_fusion), calls=%async_computation.1 | async-start | bytes 8388608 | tf_op jit(solution)/shard_map/all_to_all | solution.py:124
  33.3 0.0 copy-start
  33.3 38.3 %all_gather.3 = bf16[3072,128]{1,0:T(8,128)(2,1)S(1)} all-gather(bf16[192,128]{1,0:T(8,128)(2,1)S(1)} %constant_dynamic-slice_fusion), channel_id=1, replica_groups=mesh['section'=16,'expert'=16,'seq'=4] {'section'}, dimensions={0}, use_global_device_ids=true | all-gather | bytes 835584 | tf_op jit(solution)/shard_map/all_gather | solution.py:132
  71.6 9.6 %all-to-all-done.1.w_ref = bf16[4,2048,256]{2,1,0:T(8,128)(2,1)} async-done(((bf16[4,2048,256]{2,1,0:T(8,128)(2,1)}), bf16[4,2048,256]{2,1,0:T(8,128)(2,1)}, u32[]{:S(2)}, u32[]{:S(2)}) %all-to-all-start.1) | async-done | bytes 4194336 | tf_op jit(solution)/shard_map/all_to_all | solution.py:124
  81.2 0.0 copy-start.1
  81.2 3.2 %shard_map.64 = (f32[4,192,256]{2,1,0:T(8,128)S(1)}, bf16[4,192,256]{2,1,0:T(8,128)(2,1)S(1)}) custom-call(bf16[16,192,128]{2,1,0:T(8,128)(2,1)S(1)} %bitcast.34, bf16[4,2048,256]{2,1,0:T(8,128)(2,1)} %all-to-all-done.1.w_ref), custom_call_target="tpu_custom_call" | custom-call | tf_op jit(solution)/shard_map/pallas_call | solution.py:134
  84.4 1.9 collective-permute-start
  86.3 10.8 %collective-permute-done.got_ref = bf16[4,192,256]{2,1,0:T(8,128)(2,1)S(1)} collective-permute-done((bf16[4,192,256]{2,1,0:T(8,128)(2,1)S(1)}, bf16[4,192,256]{2,1,0:T(8,128)(2,1)S(1)}, u32[]{:S(2)}, u32[]{:S(2)}) %collective-permute-start) | collective-permute-done | bytes 393248 | tf_op jit(solution)/shard_map/ppermute | solution.py:85
  97.1 0.2 shard_map.65.own_ref
  97.3 4.0 %collective-permute-start.1 = (bf16[4,192,128]{2,1,0:T(8,128)(2,1)S(1)}, bf16[4,192,128]{2,1,0:T(8,128)(2,1)S(1)}, u32[]{:S(2)}, u32[]{:S(2)}) collective-permute-start(bf16[4,192,128]{2,1,0:T(8,128)(2,1)S(1)} %shard_map.65.own_ref), channel_id=1, source_target_pairs={{0,3},{1,2},{2,1},{3,0},{4,7},{5,6},{6,5},{7,4},{8,11},{9,10},{10,... | collective-permute-start | bytes 589832 | tf_op jit(solution)/shard_map/ppermute | solution.py:85
  101.2 4.8 %collective-permute-done.1.got_ref = bf16[4,192,128]{2,1,0:T(8,128)(2,1)S(1)} collective-permute-done((bf16[4,192,128]{2,1,0:T(8,128)(2,1)S(1)}, bf16[4,192,128]{2,1,0:T(8,128)(2,1)S(1)}, u32[]{:S(2)}, u32[]{:S(2)}) %collective-permute-start.1) | collective-permute-done | bytes 196640 | tf_op jit(solution)/shard_map/ppermute | solution.py:85
  106.1 0.0 copy-done
  106.1 1.6 shard_map.66
  107.7 10.0 %all-to-all-start.2 = ((bf16[16,192,128]{2,1,0:T(8,128)(2,1)}), bf16[16,192,128]{2,1,0:T(8,128)(2,1)S(1)}, u32[]{:S(2)}, u32[]{:S(2)}) async-start(bf16[16,192,128]{2,1,0:T(8,128)(2,1)} %shard_map.66), calls=%async_computation.2 | async-start | bytes 1572864 | tf_op jit(solution)/shard_map/all_to_all | solution.py:162
  117.8 0.0 copy-done.1
  117.8 36.7 %all-to-all-done.2.terms_ref = bf16[16,192,128]{2,1,0:T(8,128)(2,1)S(1)} async-done(((bf16[16,192,128]{2,1,0:T(8,128)(2,1)}), bf16[16,192,128]{2,1,0:T(8,128)(2,1)S(1)}, u32[]{:S(2)}, u32[]{:S(2)}) %all-to-all-start.2) | async-done | bytes 786464 | tf_op jit(solution)/shard_map/all_to_all | solution.py:162
  154.4 0.7 shard_map.67
  155.2 3.5 %all-to-all-start.3 = ((bf16[16,24,128]{2,1,0:T(8,128)(2,1)}), bf16[16,24,128]{2,1,0:T(8,128)(2,1)S(1)}, u32[]{:S(2)}, u32[]{:S(2)}) async-start(bf16[16,24,128]{2,1,0:T(8,128)(2,1)} %bitcast.16), calls=%async_computation.3 | async-start | bytes 196608 | tf_op jit(solution)/shard_map/all_to_all | solution.py:170
  158.7 0.1 subtract_convert_fusion
  158.9 8.1 %all-to-all-done.3 = bf16[16,24,128]{2,1,0:T(8,128)(2,1)S(1)} async-done(((bf16[16,24,128]{2,1,0:T(8,128)(2,1)}), bf16[16,24,128]{2,1,0:T(8,128)(2,1)S(1)}, u32[]{:S(2)}, u32[]{:S(2)}) %all-to-all-start.3) | async-done | bytes 98336 | tf_op jit(solution)/shard_map/all_to_all | solution.py:170
  166.9 0.3 shard_map.68
  167.2 26.9 %all_to_all.25.got_ref = bf16[16,64,128]{2,1,0:T(8,128)(2,1)S(1)} all-to-all(bf16[16,64,128]{2,1,0:T(8,128)(2,1)S(1)} %shard_map.68), channel_id=1, replica_groups=mesh['section'=16,'expert'=16,'seq'=4] {'section'}, dimensions={0} | all-to-all | bytes 524288 | tf_op jit(solution)/shard_map/all_to_all | solution.py:181
  194.1 0.9 shard_map.69
  (4 shorter events, 0.0 us)
Async XLA Ops:
  3.6 15.5 %all-to-all-start = ((bf16[16,24,128]{2,1,0:T(8,128)(2,1)}), bf16[16,24,128]{2,1,0:T(8,128)(2,1)S(1)}, u32[]{:S(2)}, u32[]{:S(2)}) async-start(bf16[16,24,128]{2,1,0:T(8,128)(2,1)} %bitcast.4), calls=%async_computation | async-start | bytes 196608 | tf_op jit(solution)/shard_map/all_to_all | solution.py:127
  19.2 62.0 %all-to-all-start.1 = ((bf16[4,2048,256]{2,1,0:T(8,128)(2,1)}), bf16[4,2048,256]{2,1,0:T(8,128)(2,1)}, u32[]{:S(2)}, u32[]{:S(2)}) async-start(bf16[4,2048,256]{2,1,0:T(8,128)(2,1)} %pad_maximum_fusion), calls=%async_computation.1 | async-start | bytes 8388608 | tf_op jit(solution)/shard_map/all_to_all | solution.py:124
  33.3 72.7 %copy-start = (bf16[1,512,1024]{2,1,0:T(8,128)(2,1)S(1)}, bf16[1,512,1024]{2,1,0:T(8,128)(2,1)}, u32[]{:S(2)}) copy-start(bf16[1,512,1024]{2,1,0:T(8,128)(2,1)} %param.11) | copy-start | bytes 3145732
  81.2 36.6 %copy-start.1 = (f32[128,2]{0,1:T(2,128)S(1)}, f32[128,2]{0,1:T(2,128)}, u32[]{:S(2)}) copy-start(f32[128,2]{0,1:T(2,128)} %param.8) | copy-start | bytes 3076
  84.4 12.7 %collective-permute-start = (bf16[4,192,256]{2,1,0:T(8,128)(2,1)S(1)}, bf16[4,192,256]{2,1,0:T(8,128)(2,1)S(1)}, u32[]{:S(2)}, u32[]{:S(2)}) collective-permute-start(bf16[4,192,256]{2,1,0:T(8,128)(2,1)S(1)} %get-tuple-element.14), channel_id=1, source_target_pairs={{0,1},{1,0},{2,3},{3,2},{4,5},{5,4},{6,7},{7,6},{8,9},{9,8},{10,11... | collective-permute-start | bytes 1179656 | tf_op jit(solution)/shard_map/ppermute | solution.py:85
  97.3 8.8 %collective-permute-start.1 = (bf16[4,192,128]{2,1,0:T(8,128)(2,1)S(1)}, bf16[4,192,128]{2,1,0:T(8,128)(2,1)S(1)}, u32[]{:S(2)}, u32[]{:S(2)}) collective-permute-start(bf16[4,192,128]{2,1,0:T(8,128)(2,1)S(1)} %shard_map.65.own_ref), channel_id=1, source_target_pairs={{0,3},{1,2},{2,1},{3,0},{4,7},{5,6},{6,5},{7,4},{8,11},{9,10},{10,... | collective-permute-start | bytes 589832 | tf_op jit(solution)/shard_map/ppermute | solution.py:85
  107.7 46.7 %all-to-all-start.2 = ((bf16[16,192,128]{2,1,0:T(8,128)(2,1)}), bf16[16,192,128]{2,1,0:T(8,128)(2,1)S(1)}, u32[]{:S(2)}, u32[]{:S(2)}) async-start(bf16[16,192,128]{2,1,0:T(8,128)(2,1)} %shard_map.66), calls=%async_computation.2 | async-start | bytes 1572864 | tf_op jit(solution)/shard_map/all_to_all | solution.py:162
  155.2 11.8 %all-to-all-start.3 = ((bf16[16,24,128]{2,1,0:T(8,128)(2,1)}), bf16[16,24,128]{2,1,0:T(8,128)(2,1)S(1)}, u32[]{:S(2)}, u32[]{:S(2)}) async-start(bf16[16,24,128]{2,1,0:T(8,128)(2,1)} %bitcast.16), calls=%async_computation.3 | async-start | bytes 196608 | tf_op jit(solution)/shard_map/all_to_all | solution.py:170

commit v3 on v1

--- a/solution.py
+++ b/solution.py
@@ -1,5 +1,3 @@
-import functools
-
 import jax
 import jax.numpy as jnp
 from jax import lax
@@ -8,18 +6,34 @@
 from jax.sharding import PartitionSpec as P
 
 VMEM = pl.BlockSpec(memory_space=pltpu.VMEM)
+ANY = pl.BlockSpec(memory_space=pl.ANY)
 SMEM = pl.BlockSpec(memory_space=pltpu.SMEM)
 PARAMS = pltpu.CompilerParams(vmem_limit_bytes=40 * 1024 * 1024)
+
+
+def split_kernel(which_ref, gate_ref, up_ref, same_ref, other_ref, sems):
+    units = gate_ref.shape[3]
+    copies = []
+    for out_ref, turn in ((other_ref, 1), (same_ref, 0)):
+        for k, ref in enumerate((gate_ref, up_ref)):
+            copies.append(
+                pltpu.make_async_copy(
+                    ref.at[:, which_ref[0] ^ turn], out_ref.at[:, :, k * units : (k + 1) * units], sems.at[2 * turn + k]
+                )
+            )
+    for copy in copies:
+        copy.start()
+    for copy in copies:
+        copy.wait()
 
 
 def up_kernel(x_ref, w0_ref, w1_ref, w2_ref, w3_ref, own_ref, send_ref):
     sections, _, width = x_ref.shape
     for block, w_ref in enumerate((w0_ref, w1_ref, w2_ref, w3_ref)):
         total = None
-        for s in range(sections):
-            term = jnp.dot(
-                x_ref[s], w_ref[s * width : (s + 1) * width, :], preferred_element_type=jnp.float32
-            )
+        for s in range(0, sections, 2):
+            rows = jnp.concatenate([x_ref[s], x_ref[s + 1]], axis=1)
+            term = jnp.dot(rows, w_ref[s * width : (s + 2) * width, :], preferred_element_type=jnp.float32)
             total = term if total is None else total + term
         own_ref[block] = total
         send_ref[block] = total.astype(jnp.bfloat16)
@@ -36,14 +50,29 @@
 def down_kernel(place_ref, own_ref, got_ref, down_ref, out_ref, lhs_ref):
     rows, units = own_ref.shape[1:]
     q, b = place_ref[0], place_ref[1]
-    for half, (ref, swap, turn) in enumerate(((own_ref, (0, 1, 3, 2), 0), (got_ref, (3, 2, 0, 1), 1))):
+    for ref, swap, turn in ((own_ref, (0, 1, 3, 2), 0), (got_ref, (3, 2, 0, 1), 1)):
+        row = pl.multiple_of((b ^ turn) * rows, rows)
         for block in range(4):
             unit = pl.multiple_of((q ^ swap[block]) * units, units)
-            lhs_ref[half, :, pl.ds(unit, units)] = ref[block]
-        row = pl.multiple_of((b ^ turn) * rows, rows)
-        out_ref[pl.ds(row, rows), :] = jnp.dot(
-            lhs_ref[half], down_ref[...], preferred_element_type=jnp.float32
-        ).astype(jnp.bfloat16)
+            lhs_ref[pl.ds(row, rows), pl.ds(unit, units)] = ref[block]
+    out_ref[...] = jnp.dot(lhs_ref[...], down_ref[...], preferred_element_type=jnp.float32).astype(jnp.bfloat16)
+
+
+def mix_kernel(returned_ref, high_ref, low_ref, out_ref):
+    rows = returned_ref[...]
+    out_ref[...] = (
+        jnp.dot(high_ref[...], rows, preferred_element_type=jnp.float32)
+        + jnp.dot(low_ref[...], rows, preferred_element_type=jnp.float32)
+    ).astype(jnp.bfloat16)
+
+
+def sum_kernel(terms_ref, out_ref):
+    total = terms_ref[0].astype(jnp.float32)
+    for s in range(1, terms_ref.shape[0]):
+        total = total + terms_ref[s].astype(jnp.float32)
+    total = total.astype(jnp.bfloat16)
+    for s in range(out_ref.shape[0]):
+        out_ref[s] = total
 
 
 def exchange(value, axis, flip):
@@ -60,12 +89,19 @@
     q = lax.axis_index("seq")
     a, b = (q ^ (q >> 1)) & 1, q >> 1
 
-    def half(weight, which):
-        blocks = weight[0].reshape(sections, 2, features, units)
-        return jnp.where(which == 0, blocks[:, 0], blocks[:, 1]).reshape(sections * features, units)
-
-    same = jnp.concatenate([half(gate_weight, a), half(up_weight, a)], axis=1)
-    other = jnp.concatenate([half(gate_weight, 1 - a), half(up_weight, 1 - a)], axis=1)
+    shape = jax.ShapeDtypeStruct((sections, features, 2 * units), jnp.bfloat16)
+    same, other = pl.pallas_call(
+        split_kernel,
+        out_shape=(shape, shape),
+        in_specs=[SMEM, ANY, ANY],
+        out_specs=(ANY, ANY),
+        scratch_shapes=[pltpu.SemaphoreType.DMA((4,))],
+    )(
+        a.astype(jnp.int32).reshape(1),
+        gate_weight[0].reshape(sections, 2, features, units),
+        up_weight[0].reshape(sections, 2, features, units),
+    )
+    same, other = (w.reshape(sections * features, 2 * units) for w in (same, other))
     w1 = exchange(other, "seq", 1)
     w2 = exchange(same, "seq", 3)
     w3 = exchange(other, "seq", 2)
@@ -95,6 +131,7 @@
     )
     half_rows = rows_total // 2
     kept = lax.dynamic_slice_in_dim(received.reshape(rows_total, features), b * half_rows, half_rows, 0)
+    kept, mixing_high, mixing_low = lax.optimization_barrier((kept, mixing_high, mixing_low))
     x = lax.all_gather(kept, "section", axis=0, tiled=True).reshape(sections, half_rows, features)
 
     own, send = pl.pallas_call(
@@ -121,22 +158,31 @@
         out_shape=jax.ShapeDtypeStruct((rows_total, columns), jnp.bfloat16),
         in_specs=[SMEM, VMEM, VMEM, VMEM],
         out_specs=VMEM,
-        scratch_shapes=[pltpu.VMEM((2, half_rows, 4 * units), jnp.bfloat16)],
+        scratch_shapes=[pltpu.VMEM((rows_total, 4 * units), jnp.bfloat16)],
         compiler_params=PARAMS,
     )(jnp.stack([q, b]).astype(jnp.int32), hidden, other_hidden, down_weight[0])
 
     returned = lax.all_to_all(
         partial_out.reshape(experts, capacity, columns), "expert", split_axis=0, concat_axis=0, tiled=True
     ).reshape(rows_total, columns)
-    mixed = jnp.dot(mixing_high, returned, preferred_element_type=jnp.float32) + jnp.dot(
-        mixing_low, returned, preferred_element_type=jnp.float32
-    )
+    mixed = pl.pallas_call(
+        mix_kernel,
+        out_shape=jax.ShapeDtypeStruct((tok_rows, columns), jnp.bfloat16),
+        in_specs=[VMEM] * 3,
+        out_specs=VMEM,
+        compiler_params=PARAMS,
+    )(returned, mixing_high, mixing_low)
     part = tok_rows // sections
     terms = lax.all_to_all(
-        mixed.astype(jnp.bfloat16).reshape(sections, part, columns), "section", split_axis=0, concat_axis=0, tiled=True
+        mixed.reshape(sections, part, columns), "section", split_axis=0, concat_axis=0, tiled=True
     )
-    summed = jnp.sum(terms.astype(jnp.float32), axis=0).astype(jnp.bfloat16)
-    copies = jnp.broadcast_to(summed[None], (sections, part, columns))
+    copies = pl.pallas_call(
+        sum_kernel,
+        out_shape=jax.ShapeDtypeStruct((sections, part, columns), jnp.bfloat16),
+        in_specs=[VMEM],
+        out_specs=VMEM,
+        compiler_params=PARAMS,
+    )(terms)
     return lax.all_to_all(copies, "section", split_axis=0, concat_axis=0, tiled=True).reshape(tok_rows, columns)
 
 

time: 178 us -> 235 us (1.32)
  Pallas kernels: 5.2 us -> 68.7 us
  blocking collectives: 89.8 us -> 113 us
  waiting for transfers between devices: 42.9 us -> 21.3 us
  starting transfers between devices: 32 us -> 28.6 us
  other arithmetic: 2.99 us -> 0.23 us
    pallas_call x0 -> x3, Pallas kernels: none -> 65.2 us  [the longest x1 64.7 us: shards(): pl.pallas_call(split_kernel, out_shape=(shape, shape), in_specs=[SMEM, AN...]
    all_to_all x1 -> x2, blocking collectives: 20.8 us -> 47.9 us  [the longest x1 24.9 us: shards(): lax.all_to_all(partial_out.reshape(experts, capacity, columns), 'expert',...]
    all_to_all x1 -> x0, waiting for transfers between devices: 20.6 us -> none  [shards(): lax.all_to_all(partial_out.reshape(experts, capacity, columns), 'expert',...]
    all_to_all x1, blocking collectives: 28.4 us -> 24.3 us  [shards(): lax.all_to_all(copies, 'section', split_axis=0, concat_axis=0, tiled=True)]
    all_to_all x1 -> x0, starting transfers between devices: 3.74 us -> none  [shards(): lax.all_to_all(partial_out.reshape(experts, capacity, columns), 'expert',...]
  transfers between devices with their start and end apart: 7 -> 6, of which waited for: 4 -> 3; matrix products, arithmetic and copies ran while one was open for 1% -> 1% of each run, Pallas kernels for 0% -> 0%
where the time goes in v3:
time: 235 us; the launch traced here: 234 us
  blocking collectives  113 us (48%)
  Pallas kernels  68.7 us (29%)
  starting transfers between devices  28.6 us (12%)
  waiting for transfers between devices  21.3 us (9%)
    pallas_call x1, Pallas kernels, shards(): pl.pallas_call(split_kernel, out_shape=(shape, shape), in_specs=[SMEM, AN...  64.7 us
    all_gather x1, blocking collectives, shards(): lax.all_gather(kept, 'section', axis=0, tiled=True)  41 us
    ppermute x5, starting transfers between devices, exchange(): lax.ppermute(value, axis, [(i, i ^ flip) for i in range(lax.axis_size(axi...  25.1 us
    all_to_all x1, blocking collectives, shards(): lax.all_to_all(partial_out.reshape(experts, capacity, columns), 'expert',...  24.9 us
    all_to_all x1, blocking collectives, shards(): lax.all_to_all(copies, 'section', split_axis=0, concat_axis=0, tiled=True)  24.3 us
    all_to_all x1, blocking collectives, shards(): lax.all_to_all(mixed.reshape(sections, part, columns), 'section', split_a...  23 us
    ppermute x5, waiting for transfers between devices, exchange(): lax.ppermute(value, axis, [(i, i ^ flip) for i in range(lax.axis_size(axi...  13.2 us
    all_to_all x1, waiting for transfers between devices, shards(): lax.all_to_all(outgoing.reshape(experts, capacity, features), 'expert', s...  8.07 us
  transfers between devices with their start and end apart: 6, of which 3 were waited for; matrix products, arithmetic and copies ran while one was open for 1% of the time, Pallas kernels for 0%

profile of v3, /device:TPU:6, one launch (start us, length us, event | category | flops | bytes accessed | tf_op | source)
XLA Modules:
  0.0 234.4 jit_solution(11461464436129458490)
XLA Ops:
  0.0 0.0 copy-start.2
  0.0 0.0 copy-start.4
  0.0 0.0 copy-start.3
  0.0 64.7 %shard_map.64 = (bf16[16,128,256]{2,1,0:T(8,128)(2,1)}, bf16[16,128,256]{2,1,0:T(8,128)(2,1)}) custom-call(s32[1]{0:T(128)} %bitcast.9.which_ref, bf16[16,2,128,128]{3,2,1,0:T(8,128)(2,1)} %bitcast.30, bf16[16,2,128,128]{3,2,1,0:T(8,128)(2,1)} %bitcast.31), custom_call_target="tpu_custom_call" | custom-call | tf_op jit(solution)/shard_map/pallas_call | solution.py:93
  64.7 0.0 copy-start
  64.7 3.4 %collective-permute-start.2 = (bf16[2048,256]{1,0:T(8,128)(2,1)}, bf16[2048,256]{1,0:T(8,128)(2,1)S(1)}, u32[]{:S(2)}, u32[]{:S(2)}) collective-permute-start(bf16[2048,256]{1,0:T(8,128)(2,1)} %bitcast.34), channel_id=1, source_target_pairs={{0,2},{1,3},{2,0},{3,1},{4,6},{5,7},{6,4},{7,5},{8,10},{9,11},{10,... | collective-permute-start | bytes 3145736 | tf_op jit(solution)/shard_map/ppermute | solution.py:79
  68.2 14.5 %collective-permute-start = (bf16[2048,256]{1,0:T(8,128)(2,1)}, bf16[2048,256]{1,0:T(8,128)(2,1)S(1)}, u32[]{:S(2)}, u32[]{:S(2)}) collective-permute-start(bf16[2048,256]{1,0:T(8,128)(2,1)} %bitcast.35), channel_id=1, source_target_pairs={{0,1},{1,0},{2,3},{3,2},{4,5},{5,4},{6,7},{7,6},{8,9},{9,8},{10,11... | collective-permute-start | bytes 3145736 | tf_op jit(solution)/shard_map/ppermute | solution.py:79
  82.6 1.9 collective-permute-start.1
  84.6 0.0 copy-done.2
  84.6 0.1 copy.13
  84.7 0.1 eq.75
  84.8 0.2 fusion
  85.1 0.1 convert_element_type.28
  85.2 0.1 copy.14
  85.3 0.0 copy-done.4
  85.3 0.8 convolution_convert_fusion
  86.1 3.5 %all-to-all-start = ((bf16[16,24,128]{2,1,0:T(8,128)(2,1)}), bf16[16,24,128]{2,1,0:T(8,128)(2,1)S(1)}, u32[]{:S(2)}, u32[]{:S(2)}) async-start(bf16[16,24,128]{2,1,0:T(8,128)(2,1)} %bitcast.4), calls=%async_computation | async-start | bytes 196608 | tf_op jit(solution)/shard_map/all_to_all | solution.py:129
  89.6 0.0 copy-done.3
  89.7 0.1 subtract_convert_fusion
  89.8 8.1 %all-to-all-done = bf16[16,24,128]{2,1,0:T(8,128)(2,1)S(1)} async-done(((bf16[16,24,128]{2,1,0:T(8,128)(2,1)}), bf16[16,24,128]{2,1,0:T(8,128)(2,1)S(1)}, u32[]{:S(2)}, u32[]{:S(2)}) %all-to-all-start) | async-done | bytes 98336 | tf_op jit(solution)/shard_map/all_to_all | solution.py:129
  97.9 41.0 %all_gather.3 = bf16[3072,128]{1,0:T(8,128)(2,1)S(1)} all-gather(bf16[192,128]{1,0:T(8,128)(2,1)S(1)} %constant_dynamic-slice_fusion), channel_id=1, replica_groups=mesh['section'=16,'expert'=16,'seq'=4] {'section'}, dimensions={0}, use_global_device_ids=true | all-gather | bytes 835584 | tf_op jit(solution)/shard_map/all_gather | solution.py:135
  138.9 0.0 collective-permute-done.2.w3_ref
  138.9 0.0 collective-permute-done.w1_ref
  138.9 0.0 collective-permute-done.1.w2_ref
  138.9 0.0 copy-done
  138.9 2.2 shard_map.65
  141.1 0.0 copy-start.1
  141.1 2.8 %collective-permute-start.3 = (bf16[4,192,256]{2,1,0:T(8,128)(2,1)S(1)}, bf16[4,192,256]{2,1,0:T(8,128)(2,1)S(1)}, u32[]{:S(2)}, u32[]{:S(2)}) collective-permute-start(bf16[4,192,256]{2,1,0:T(8,128)(2,1)S(1)} %get-tuple-element.16), channel_id=1, source_target_pairs={{0,1},{1,0},{2,3},{3,2},{4,5},{5,4},{6,7},{7,6},{8,9},{9,8},{10,11... | collective-permute-start | bytes 1179656 | tf_op jit(solution)/shard_map/ppermute | solution.py:79
  144.0 7.0 %collective-permute-done.3.got_ref = bf16[4,192,256]{2,1,0:T(8,128)(2,1)S(1)} collective-permute-done((bf16[4,192,256]{2,1,0:T(8,128)(2,1)S(1)}, bf16[4,192,256]{2,1,0:T(8,128)(2,1)S(1)}, u32[]{:S(2)}, u32[]{:S(2)}) %collective-permute-start.3) | collective-permute-done | bytes 393248 | tf_op jit(solution)/shard_map/ppermute | solution.py:79
  150.9 0.2 shard_map.66.own_ref
  151.1 2.5 %collective-permute-start.4 = (bf16[4,192,128]{2,1,0:T(8,128)(2,1)S(1)}, bf16[4,192,128]{2,1,0:T(8,128)(2,1)S(1)}, u32[]{:S(2)}, u32[]{:S(2)}) collective-permute-start(bf16[4,192,128]{2,1,0:T(8,128)(2,1)S(1)} %shard_map.66.own_ref), channel_id=1, source_target_pairs={{0,3},{1,2},{2,1},{3,0},{4,7},{5,6},{6,5},{7,4},{8,11},{9,10},{10,... | collective-permute-start | bytes 589832 | tf_op jit(solution)/shard_map/ppermute | solution.py:79
  153.6 0.1 pad_add_fusion.place_ref
  153.7 6.2 %collective-permute-done.4.got_ref = bf16[4,192,128]{2,1,0:T(8,128)(2,1)S(1)} collective-permute-done((bf16[4,192,128]{2,1,0:T(8,128)(2,1)S(1)}, bf16[4,192,128]{2,1,0:T(8,128)(2,1)S(1)}, u32[]{:S(2)}, u32[]{:S(2)}) %collective-permute-start.4) | collective-permute-done | bytes 196640 | tf_op jit(solution)/shard_map/ppermute | solution.py:79
  159.9 0.0 copy-done.1
  159.9 1.2 shard_map.67
  161.0 24.9 %all_to_all.20 = bf16[16,24,1024]{2,1,0:T(8,128)(2,1)S(1)} all-to-all(bf16[16,24,1024]{2,1,0:T(8,128)(2,1)S(1)} %bitcast.24), channel_id=1, replica_groups=mesh['section'=16,'expert'=16,'seq'=4] {'expert'}, dimensions={0} | all-to-all | bytes 1572864 | tf_op jit(solution)/shard_map/all_to_all | solution.py:165
  185.9 0.4 shard_map.68
  186.4 23.0 %all_to_all.21.terms_ref = bf16[16,8,1024]{2,1,0:T(8,128)(2,1)S(1)} all-to-all(bf16[16,8,1024]{2,1,0:T(8,128)(2,1)S(1)} %bitcast.29), channel_id=1, replica_groups=mesh['section'=16,'expert'=16,'seq'=4] {'section'}, dimensions={0} | all-to-all | bytes 524288 | tf_op jit(solution)/shard_map/all_to_all | solution.py:176
  209.4 24.3 %all_to_all.22 = bf16[16,8,1024]{2,1,0:T(8,128)(2,1)S(1)} all-to-all(bf16[16,8,1024]{2,1,0:T(8,128)(2,1)S(1)} %shard_map.69), channel_id=1, replica_groups=mesh['section'=16,'expert'=16,'seq'=4] {'section'}, dimensions={0} | all-to-all | bytes 524288 | tf_op jit(solution)/shard_map/all_to_all | solution.py:186
  233.7 0.7 copy.16
  (6 shorter events, 0.1 us)
Async XLA Ops:
  0.0 84.6 %copy-start.2 = (s32[128,2]{0,1:T(2,128)S(1)}, s32[128,2]{0,1:T(2,128)}, u32[]{:S(2)}) copy-start(s32[128,2]{0,1:T(2,128)} %param.7) | copy-start | bytes 3076
  0.0 85.3 %copy-start.4 = (bf16[128,256]{1,0:T(8,128)(2,1)S(1)}, bf16[128,256]{1,0:T(8,128)(2,1)}, u32[]{:S(2)}) copy-start(bf16[128,256]{1,0:T(8,128)(2,1)} %param.6) | copy-start | bytes 196612
  0.0 89.6 %copy-start.3 = (f32[128,2]{0,1:T(2,128)S(1)}, f32[128,2]{0,1:T(2,128)}, u32[]{:S(2)}) copy-start(f32[128,2]{0,1:T(2,128)} %param.8) | copy-start | bytes 3076
  64.7 74.2 %copy-start = (bf16[16,128,256]{2,1,0:T(8,128)(2,1)S(1)}, bf16[16,128,256]{2,1,0:T(8,128)(2,1)}, u32[]{:S(2)}) copy-start(bf16[16,128,256]{2,1,0:T(8,128)(2,1)} %get-tuple-element.13) | copy-start | bytes 3145732
  64.7 74.2 %collective-permute-start.2 = (bf16[2048,256]{1,0:T(8,128)(2,1)}, bf16[2048,256]{1,0:T(8,128)(2,1)S(1)}, u32[]{:S(2)}, u32[]{:S(2)}) collective-permute-start(bf16[2048,256]{1,0:T(8,128)(2,1)} %bitcast.34), channel_id=1, source_target_pairs={{0,2},{1,3},{2,0},{3,1},{4,6},{5,7},{6,4},{7,5},{8,10},{9,11},{10,... | collective-permute-start | bytes 3145736 | tf_op jit(solution)/shard_map/ppermute | solution.py:79
  68.2 70.7 %collective-permute-start = (bf16[2048,256]{1,0:T(8,128)(2,1)}, bf16[2048,256]{1,0:T(8,128)(2,1)S(1)}, u32[]{:S(2)}, u32[]{:S(2)}) collective-permute-start(bf16[2048,256]{1,0:T(8,128)(2,1)} %bitcast.35), channel_id=1, source_target_pairs={{0,1},{1,0},{2,3},{3,2},{4,5},{5,4},{6,7},{7,6},{8,9},{9,8},{10,11... | collective-permute-start | bytes 3145736 | tf_op jit(solution)/shard_map/ppermute | solution.py:79
  82.6 56.3 %collective-permute-start.1 = (bf16[2048,256]{1,0:T(8,128)(2,1)}, bf16[2048,256]{1,0:T(8,128)(2,1)}, u32[]{:S(2)}, u32[]{:S(2)}) collective-permute-start(bf16[2048,256]{1,0:T(8,128)(2,1)} %bitcast.26), channel_id=1, source_target_pairs={{0,3},{1,2},{2,1},{3,0},{4,7},{5,6},{6,5},{7,4},{8,11},{9,10},{10,... | collective-permute-start | bytes 3145736 | tf_op jit(solution)/shard_map/ppermute | solution.py:79
  86.1 11.8 %all-to-all-start = ((bf16[16,24,128]{2,1,0:T(8,128)(2,1)}), bf16[16,24,128]{2,1,0:T(8,128)(2,1)S(1)}, u32[]{:S(2)}, u32[]{:S(2)}) async-start(bf16[16,24,128]{2,1,0:T(8,128)(2,1)} %bitcast.4), calls=%async_computation | async-start | bytes 196608 | tf_op jit(solution)/shard_map/all_to_all | solution.py:129
  141.1 18.8 %copy-start.1 = (bf16[1,512,1024]{2,1,0:T(8,128)(2,1)S(1)}, bf16[1,512,1024]{2,1,0:T(8,128)(2,1)}, u32[]{:S(2)}) copy-start(bf16[1,512,1024]{2,1,0:T(8,128)(2,1)} %param.11) | copy-start | bytes 3145732
  141.1 9.8 %collective-permute-start.3 = (bf16[4,192,256]{2,1,0:T(8,128)(2,1)S(1)}, bf16[4,192,256]{2,1,0:T(8,128)(2,1)S(1)}, u32[]{:S(2)}, u32[]{:S(2)}) collective-permute-start(bf16[4,192,256]{2,1,0:T(8,128)(2,1)S(1)} %get-tuple-element.16), channel_id=1, source_target_pairs={{0,1},{1,0},{2,3},{3,2},{4,5},{5,4},{6,7},{7,6},{8,9},{9,8},{10,11... | collective-permute-start | bytes 1179656 | tf_op jit(solution)/shard_map/ppermute | solution.py:79
  151.1 8.8 %collective-permute-start.4 = (bf16[4,192,128]{2,1,0:T(8,128)(2,1)S(1)}, bf16[4,192,128]{2,1,0:T(8,128)(2,1)S(1)}, u32[]{:S(2)}, u32[]{:S(2)}) collective-permute-start(bf16[4,192,128]{2,1,0:T(8,128)(2,1)S(1)} %shard_map.66.own_ref), channel_id=1, source_target_pairs={{0,3},{1,2},{2,1},{3,0},{4,7},{5,6},{6,5},{7,4},{8,11},{9,10},{10,... | collective-permute-start | bytes 589832 | tf_op jit(solution)/shard_map/ppermute | solution.py:79

commit v4 on v3

--- a/solution.py
+++ b/solution.py
@@ -94,7 +94,7 @@
         split_kernel,
         out_shape=(shape, shape),
         in_specs=[SMEM, ANY, ANY],
-        out_specs=(ANY, ANY),
+        out_specs=(VMEM, VMEM),
         scratch_shapes=[pltpu.SemaphoreType.DMA((4,))],
     )(
         a.astype(jnp.int32).reshape(1),

time: 235 us -> 173 us (0.74)
  Pallas kernels: 68.7 us -> 6.97 us
    pallas_call x1, Pallas kernels: 64.7 us -> 2.95 us  [shards(): pl.pallas_call(split_kernel, out_shape=(shape, shape), in_specs=[SMEM, AN...]
where the time goes in v4:
time: 173 us
  blocking collectives  113 us (65%)
  starting transfers between devices  28.6 us (17%)
  waiting for transfers between devices  21.3 us (12%)
  Pallas kernels  6.97 us (4%)
    all_gather x1, blocking collectives, shards(): lax.all_gather(kept, 'section', axis=0, tiled=True)  41 us
    ppermute x5, starting transfers between devices, exchange(): lax.ppermute(value, axis, [(i, i ^ flip) for i in range(lax.axis_size(axi...  25.1 us
    all_to_all x1, blocking collectives, shards(): lax.all_to_all(partial_out.reshape(experts, capacity, columns), 'expert',...  24.9 us
    all_to_all x1, blocking collectives, shards(): lax.all_to_all(copies, 'section', split_axis=0, concat_axis=0, tiled=True)  24.3 us
    all_to_all x1, blocking collectives, shards(): lax.all_to_all(mixed.reshape(sections, part, columns), 'section', split_a...  23 us
    ppermute x5, waiting for transfers between devices, exchange(): lax.ppermute(value, axis, [(i, i ^ flip) for i in range(lax.axis_size(axi...  13.2 us
    all_to_all x1, waiting for transfers between devices, shards(): lax.all_to_all(outgoing.reshape(experts, capacity, features), 'expert', s...  8.07 us
    all_to_all x1, starting transfers between devices, shards(): lax.all_to_all(outgoing.reshape(experts, capacity, features), 'expert', s...  3.51 us
  transfers between devices with their start and end apart: 6, of which 3 were waited for; matrix products, arithmetic and copies ran while one was open for 1% of the time, Pallas kernels for 0%

profile of v4, /device:TPU:6, one launch (start us, length us, event | category | flops | bytes accessed | tf_op | source)
XLA Modules:
  0.0 172.7 jit_solution(5408263870324289189)
XLA Ops:
  0.0 0.0 copy-start.2
  0.0 0.0 copy-start.4
  0.0 0.0 copy-start.3
  0.0 2.9 %shard_map.64 = (bf16[16,128,256]{2,1,0:T(8,128)(2,1)}, bf16[16,128,256]{2,1,0:T(8,128)(2,1)}) custom-call(s32[1]{0:T(128)} %bitcast.9.which_ref, bf16[16,2,128,128]{3,2,1,0:T(8,128)(2,1)} %bitcast.30, bf16[16,2,128,128]{3,2,1,0:T(8,128)(2,1)} %bitcast.31), custom_call_target="tpu_custom_call" | custom-call | tf_op jit(solution)/shard_map/pallas_call | solution.py:93
  3.0 0.0 copy-start
  3.0 3.4 %collective-permute-start.2 = (bf16[2048,256]{1,0:T(8,128)(2,1)}, bf16[2048,256]{1,0:T(8,128)(2,1)S(1)}, u32[]{:S(2)}, u32[]{:S(2)}) collective-permute-start(bf16[2048,256]{1,0:T(8,128)(2,1)} %bitcast.34), channel_id=1, source_target_pairs={{0,2},{1,3},{2,0},{3,1},{4,6},{5,7},{6,4},{7,5},{8,10},{9,11},{10,... | collective-permute-start | bytes 3145736 | tf_op jit(solution)/shard_map/ppermute | solution.py:79
  6.4 14.5 %collective-permute-start = (bf16[2048,256]{1,0:T(8,128)(2,1)}, bf16[2048,256]{1,0:T(8,128)(2,1)S(1)}, u32[]{:S(2)}, u32[]{:S(2)}) collective-permute-start(bf16[2048,256]{1,0:T(8,128)(2,1)} %bitcast.35), channel_id=1, source_target_pairs={{0,1},{1,0},{2,3},{3,2},{4,5},{5,4},{6,7},{7,6},{8,9},{9,8},{10,11... | collective-permute-start | bytes 3145736 | tf_op jit(solution)/shard_map/ppermute | solution.py:79
  20.9 1.9 %collective-permute-start.1 = (bf16[2048,256]{1,0:T(8,128)(2,1)}, bf16[2048,256]{1,0:T(8,128)(2,1)}, u32[]{:S(2)}, u32[]{:S(2)}) collective-permute-start(bf16[2048,256]{1,0:T(8,128)(2,1)} %bitcast.26), channel_id=1, source_target_pairs={{0,3},{1,2},{2,1},{3,0},{4,7},{5,6},{6,5},{7,4},{8,11},{9,10},{10,... | collective-permute-start | bytes 3145736 | tf_op jit(solution)/shard_map/ppermute | solution.py:79
  22.8 0.0 copy-done.2
  22.8 0.1 copy.13
  23.0 0.1 eq.75
  23.1 0.2 fusion
  23.3 0.1 convert_element_type.28
  23.5 0.1 copy.14
  23.5 0.0 copy-done.4
  23.6 0.8 convolution_convert_fusion
  24.4 3.5 %all-to-all-start = ((bf16[16,24,128]{2,1,0:T(8,128)(2,1)}), bf16[16,24,128]{2,1,0:T(8,128)(2,1)S(1)}, u32[]{:S(2)}, u32[]{:S(2)}) async-start(bf16[16,24,128]{2,1,0:T(8,128)(2,1)} %bitcast.4), calls=%async_computation | async-start | bytes 196608 | tf_op jit(solution)/shard_map/all_to_all | solution.py:129
  27.9 0.0 copy-done.3
  27.9 0.1 subtract_convert_fusion
  28.1 8.1 %all-to-all-done = bf16[16,24,128]{2,1,0:T(8,128)(2,1)S(1)} async-done(((bf16[16,24,128]{2,1,0:T(8,128)(2,1)}), bf16[16,24,128]{2,1,0:T(8,128)(2,1)S(1)}, u32[]{:S(2)}, u32[]{:S(2)}) %all-to-all-start) | async-done | bytes 98336 | tf_op jit(solution)/shard_map/all_to_all | solution.py:129
  36.1 41.0 %all_gather.3 = bf16[3072,128]{1,0:T(8,128)(2,1)S(1)} all-gather(bf16[192,128]{1,0:T(8,128)(2,1)S(1)} %constant_dynamic-slice_fusion), channel_id=1, replica_groups=mesh['section'=16,'expert'=16,'seq'=4] {'section'}, dimensions={0}, use_global_device_ids=true | all-gather | bytes 835584 | tf_op jit(solution)/shard_map/all_gather | solution.py:135
  77.2 0.0 collective-permute-done.2.w3_ref
  77.2 0.0 collective-permute-done.w1_ref
  77.2 0.0 collective-permute-done.1.w2_ref
  77.2 0.0 copy-done
  77.2 2.2 %shard_map.65 = (f32[4,192,256]{2,1,0:T(8,128)S(1)}, bf16[4,192,256]{2,1,0:T(8,128)(2,1)S(1)}) custom-call(bf16[16,192,128]{2,1,0:T(8,128)(2,1)S(1)} %bitcast.23, bf16[2048,256]{1,0:T(8,128)(2,1)S(1)} %bitcast.27, bf16[2048,256]{1,0:T(8,128)(2,1)S(1)} %collective-permute-done.w1_ref, bf16[2048,256]{1,0:T(8,128)(2,1)} %collective-permute-done.1.w2_ref, ...), custom_call_target="tpu_custom_call" | custom-call | tf_op jit(solution)/shard_map/pallas_call | solution.py:137
  79.4 0.0 copy-start.1
  79.4 2.8 %collective-permute-start.3 = (bf16[4,192,256]{2,1,0:T(8,128)(2,1)S(1)}, bf16[4,192,256]{2,1,0:T(8,128)(2,1)S(1)}, u32[]{:S(2)}, u32[]{:S(2)}) collective-permute-start(bf16[4,192,256]{2,1,0:T(8,128)(2,1)S(1)} %get-tuple-element.16), channel_id=1, source_target_pairs={{0,1},{1,0},{2,3},{3,2},{4,5},{5,4},{6,7},{7,6},{8,9},{9,8},{10,11... | collective-permute-start | bytes 1179656 | tf_op jit(solution)/shard_map/ppermute | solution.py:79
  82.2 7.0 %collective-permute-done.3.got_ref = bf16[4,192,256]{2,1,0:T(8,128)(2,1)S(1)} collective-permute-done((bf16[4,192,256]{2,1,0:T(8,128)(2,1)S(1)}, bf16[4,192,256]{2,1,0:T(8,128)(2,1)S(1)}, u32[]{:S(2)}, u32[]{:S(2)}) %collective-permute-start.3) | collective-permute-done | bytes 393248 | tf_op jit(solution)/shard_map/ppermute | solution.py:79
  89.2 0.2 shard_map.66.own_ref
  89.4 2.5 %collective-permute-start.4 = (bf16[4,192,128]{2,1,0:T(8,128)(2,1)S(1)}, bf16[4,192,128]{2,1,0:T(8,128)(2,1)S(1)}, u32[]{:S(2)}, u32[]{:S(2)}) collective-permute-start(bf16[4,192,128]{2,1,0:T(8,128)(2,1)S(1)} %shard_map.66.own_ref), channel_id=1, source_target_pairs={{0,3},{1,2},{2,1},{3,0},{4,7},{5,6},{6,5},{7,4},{8,11},{9,10},{10,... | collective-permute-start | bytes 589832 | tf_op jit(solution)/shard_map/ppermute | solution.py:79
  91.9 0.1 pad_add_fusion.place_ref
  91.9 6.2 %collective-permute-done.4.got_ref = bf16[4,192,128]{2,1,0:T(8,128)(2,1)S(1)} collective-permute-done((bf16[4,192,128]{2,1,0:T(8,128)(2,1)S(1)}, bf16[4,192,128]{2,1,0:T(8,128)(2,1)S(1)}, u32[]{:S(2)}, u32[]{:S(2)}) %collective-permute-start.4) | collective-permute-done | bytes 196640 | tf_op jit(solution)/shard_map/ppermute | solution.py:79
  98.2 0.0 copy-done.1
  98.2 1.2 shard_map.67
  99.3 24.9 %all_to_all.20 = bf16[16,24,1024]{2,1,0:T(8,128)(2,1)S(1)} all-to-all(bf16[16,24,1024]{2,1,0:T(8,128)(2,1)S(1)} %bitcast.24), channel_id=1, replica_groups=mesh['section'=16,'expert'=16,'seq'=4] {'expert'}, dimensions={0} | all-to-all | bytes 1572864 | tf_op jit(solution)/shard_map/all_to_all | solution.py:165
  124.2 0.5 shard_map.68
  124.7 23.0 %all_to_all.21.terms_ref = bf16[16,8,1024]{2,1,0:T(8,128)(2,1)S(1)} all-to-all(bf16[16,8,1024]{2,1,0:T(8,128)(2,1)S(1)} %bitcast.29), channel_id=1, replica_groups=mesh['section'=16,'expert'=16,'seq'=4] {'section'}, dimensions={0} | all-to-all | bytes 524288 | tf_op jit(solution)/shard_map/all_to_all | solution.py:176
  147.7 24.3 %all_to_all.22 = bf16[16,8,1024]{2,1,0:T(8,128)(2,1)S(1)} all-to-all(bf16[16,8,1024]{2,1,0:T(8,128)(2,1)S(1)} %shard_map.69), channel_id=1, replica_groups=mesh['section'=16,'expert'=16,'seq'=4] {'section'}, dimensions={0} | all-to-all | bytes 524288 | tf_op jit(solution)/shard_map/all_to_all | solution.py:186
  172.0 0.7 copy.16
  (6 shorter events, 0.1 us)
Async XLA Ops:
  0.0 22.8 %copy-start.2 = (s32[128,2]{0,1:T(2,128)S(1)}, s32[128,2]{0,1:T(2,128)}, u32[]{:S(2)}) copy-start(s32[128,2]{0,1:T(2,128)} %param.7) | copy-start | bytes 3076
  0.0 23.5 %copy-start.4 = (bf16[128,256]{1,0:T(8,128)(2,1)S(1)}, bf16[128,256]{1,0:T(8,128)(2,1)}, u32[]{:S(2)}) copy-start(bf16[128,256]{1,0:T(8,128)(2,1)} %param.6) | copy-start | bytes 196612
  0.0 27.9 %copy-start.3 = (f32[128,2]{0,1:T(2,128)S(1)}, f32[128,2]{0,1:T(2,128)}, u32[]{:S(2)}) copy-start(f32[128,2]{0,1:T(2,128)} %param.8) | copy-start | bytes 3076
  3.0 74.2 %copy-start = (bf16[16,128,256]{2,1,0:T(8,128)(2,1)S(1)}, bf16[16,128,256]{2,1,0:T(8,128)(2,1)}, u32[]{:S(2)}) copy-start(bf16[16,128,256]{2,1,0:T(8,128)(2,1)} %get-tuple-element.13) | copy-start | bytes 3145732
  3.0 74.2 %collective-permute-start.2 = (bf16[2048,256]{1,0:T(8,128)(2,1)}, bf16[2048,256]{1,0:T(8,128)(2,1)S(1)}, u32[]{:S(2)}, u32[]{:S(2)}) collective-permute-start(bf16[2048,256]{1,0:T(8,128)(2,1)} %bitcast.34), channel_id=1, source_target_pairs={{0,2},{1,3},{2,0},{3,1},{4,6},{5,7},{6,4},{7,5},{8,10},{9,11},{10,... | collective-permute-start | bytes 3145736 | tf_op jit(solution)/shard_map/ppermute | solution.py:79
  6.4 70.7 %collective-permute-start = (bf16[2048,256]{1,0:T(8,128)(2,1)}, bf16[2048,256]{1,0:T(8,128)(2,1)S(1)}, u32[]{:S(2)}, u32[]{:S(2)}) collective-permute-start(bf16[2048,256]{1,0:T(8,128)(2,1)} %bitcast.35), channel_id=1, source_target_pairs={{0,1},{1,0},{2,3},{3,2},{4,5},{5,4},{6,7},{7,6},{8,9},{9,8},{10,11... | collective-permute-start | bytes 3145736 | tf_op jit(solution)/shard_map/ppermute | solution.py:79
  20.9 56.3 %collective-permute-start.1 = (bf16[2048,256]{1,0:T(8,128)(2,1)}, bf16[2048,256]{1,0:T(8,128)(2,1)}, u32[]{:S(2)}, u32[]{:S(2)}) collective-permute-start(bf16[2048,256]{1,0:T(8,128)(2,1)} %bitcast.26), channel_id=1, source_target_pairs={{0,3},{1,2},{2,1},{3,0},{4,7},{5,6},{6,5},{7,4},{8,11},{9,10},{10,... | collective-permute-start | bytes 3145736 | tf_op jit(solution)/shard_map/ppermute | solution.py:79
  24.4 11.8 %all-to-all-start = ((bf16[16,24,128]{2,1,0:T(8,128)(2,1)}), bf16[16,24,128]{2,1,0:T(8,128)(2,1)S(1)}, u32[]{:S(2)}, u32[]{:S(2)}) async-start(bf16[16,24,128]{2,1,0:T(8,128)(2,1)} %bitcast.4), calls=%async_computation | async-start | bytes 196608 | tf_op jit(solution)/shard_map/all_to_all | solution.py:129
  79.4 18.8 %copy-start.1 = (bf16[1,512,1024]{2,1,0:T(8,128)(2,1)S(1)}, bf16[1,512,1024]{2,1,0:T(8,128)(2,1)}, u32[]{:S(2)}) copy-start(bf16[1,512,1024]{2,1,0:T(8,128)(2,1)} %param.11) | copy-start | bytes 3145732
  79.4 9.8 %collective-permute-start.3 = (bf16[4,192,256]{2,1,0:T(8,128)(2,1)S(1)}, bf16[4,192,256]{2,1,0:T(8,128)(2,1)S(1)}, u32[]{:S(2)}, u32[]{:S(2)}) collective-permute-start(bf16[4,192,256]{2,1,0:T(8,128)(2,1)S(1)} %get-tuple-element.16), channel_id=1, source_target_pairs={{0,1},{1,0},{2,3},{3,2},{4,5},{5,4},{6,7},{7,6},{8,9},{9,8},{10,11... | collective-permute-start | bytes 1179656 | tf_op jit(solution)/shard_map/ppermute | solution.py:79
  89.4 8.8 %collective-permute-start.4 = (bf16[4,192,128]{2,1,0:T(8,128)(2,1)S(1)}, bf16[4,192,128]{2,1,0:T(8,128)(2,1)S(1)}, u32[]{:S(2)}, u32[]{:S(2)}) collective-permute-start(bf16[4,192,128]{2,1,0:T(8,128)(2,1)S(1)} %shard_map.66.own_ref), channel_id=1, source_target_pairs={{0,3},{1,2},{2,1},{3,0},{4,7},{5,6},{6,5},{7,4},{8,11},{9,10},{10,... | collective-permute-start | bytes 589832 | tf_op jit(solution)/shard_map/ppermute | solution.py:79

commit v5 on v4

--- a/solution.py
+++ b/solution.py
@@ -11,20 +11,53 @@
 PARAMS = pltpu.CompilerParams(vmem_limit_bytes=40 * 1024 * 1024)
 
 
-def split_kernel(which_ref, gate_ref, up_ref, same_ref, other_ref, sems):
-    units = gate_ref.shape[3]
-    copies = []
-    for out_ref, turn in ((other_ref, 1), (same_ref, 0)):
-        for k, ref in enumerate((gate_ref, up_ref)):
-            copies.append(
-                pltpu.make_async_copy(
-                    ref.at[:, which_ref[0] ^ turn], out_ref.at[:, :, k * units : (k + 1) * units], sems.at[2 * turn + k]
-                )
-            )
+def front_kernel(
+    which_ref, ids_ref, tokens_ref, gate_ref, up_ref, same_ref, other_ref, rows_ref, place_ref, stage_ref, in_sems, out_sems
+):
+    units, features = gate_ref.shape[3], gate_ref.shape[2]
+    which = which_ref[0]
+    copies = [
+        pltpu.make_async_copy(
+            ref.at[:, which ^ turn], stage_ref.at[turn, :, :, k * units : (k + 1) * units], in_sems.at[2 * turn + k]
+        )
+        for turn in (1, 0)
+        for k, ref in enumerate((gate_ref, up_ref))
+    ]
     for copy in copies:
         copy.start()
-    for copy in copies:
-        copy.wait()
+
+    experts = which_ref.shape[0]
+    top_count, count = ids_ref.shape
+    rows_total = rows_ref.shape[0]
+    capacity = rows_total // experts
+    expert = lax.broadcasted_iota(jnp.int32, (experts, count), 0)
+    ids = [ids_ref[k : k + 1, :] for k in range(top_count)]
+    named = [jnp.where(expert == i, 1.0, 0.0) for i in ids]
+    before = lax.broadcasted_iota(jnp.int32, (count, count), 0) < lax.broadcasted_iota(jnp.int32, (count, count), 1)
+    earlier = jnp.dot(
+        sum(named).astype(jnp.bfloat16),
+        jnp.where(before, 1.0, 0.0).astype(jnp.bfloat16),
+        preferred_element_type=jnp.float32,
+    )
+    row = lax.broadcasted_iota(jnp.int32, (rows_total, count), 0)
+    dispatch = jnp.zeros((rows_total, count), jnp.float32)
+    for k in range(top_count):
+        slot = jnp.sum(named[k] * earlier, axis=0, keepdims=True).astype(jnp.int32)
+        place = ids[k] * capacity + slot
+        place_ref[k : k + 1, :] = place
+        dispatch = dispatch + jnp.where(row == place, 1.0, 0.0)
+    mine = tokens_ref[:, pl.ds(pl.multiple_of(which * features, features), features)]
+    rows_ref[...] = jnp.dot(dispatch.astype(jnp.bfloat16), mine, preferred_element_type=jnp.float32).astype(jnp.bfloat16)
+
+    outs = [
+        pltpu.make_async_copy(stage_ref.at[turn], ref, out_sems.at[turn]) for turn, ref in ((1, other_ref), (0, same_ref))
+    ]
+    for k, out in enumerate(outs):
+        copies[2 * k].wait()
+        copies[2 * k + 1].wait()
+        out.start()
+    for out in outs:
+        out.wait()
 
 
 def up_kernel(x_ref, w0_ref, w1_ref, w2_ref, w3_ref, own_ref, send_ref):
@@ -90,14 +123,25 @@
     a, b = (q ^ (q >> 1)) & 1, q >> 1
 
     shape = jax.ShapeDtypeStruct((sections, features, 2 * units), jnp.bfloat16)
-    same, other = pl.pallas_call(
-        split_kernel,
-        out_shape=(shape, shape),
-        in_specs=[SMEM, ANY, ANY],
-        out_specs=(VMEM, VMEM),
-        scratch_shapes=[pltpu.SemaphoreType.DMA((4,))],
+    same, other, outgoing, destination = pl.pallas_call(
+        front_kernel,
+        out_shape=(
+            shape,
+            shape,
+            jax.ShapeDtypeStruct((rows_total, features), jnp.bfloat16),
+            jax.ShapeDtypeStruct((top_count, tok_rows), jnp.int32),
+        ),
+        in_specs=[SMEM, VMEM, VMEM, ANY, ANY],
+        out_specs=(ANY, ANY, VMEM, VMEM),
+        scratch_shapes=[
+            pltpu.VMEM((2, sections, features, 2 * units), jnp.bfloat16),
+            pltpu.SemaphoreType.DMA((4,)),
+            pltpu.SemaphoreType.DMA((2,)),
+        ],
     )(
-        a.astype(jnp.int32).reshape(1),
+        jnp.broadcast_to(a.astype(jnp.int32), (experts,)),
+        route_ids.T,
+        tokens,
         gate_weight[0].reshape(sections, 2, features, units),
         up_weight[0].reshape(sections, 2, features, units),
     )
@@ -106,17 +150,8 @@
     w2 = exchange(same, "seq", 3)
     w3 = exchange(other, "seq", 2)
 
-    flat_ids = route_ids.reshape(-1)
-    pairs = tok_rows * top_count
-    onehot = flat_ids[:, None] == jnp.arange(experts, dtype=jnp.int32)[None, :]
-    order = jnp.arange(pairs, dtype=jnp.int32)
-    below = (order[:, None] > order[None, :]).astype(jnp.bfloat16)
-    earlier = jnp.dot(below, onehot.astype(jnp.bfloat16), preferred_element_type=jnp.float32)
-    slot_index = jnp.sum(jnp.where(onehot, earlier, 0.0), axis=1).astype(jnp.int32)
-    destination = (flat_ids * capacity + slot_index).reshape(tok_rows, top_count)
     place = jnp.arange(rows_total, dtype=jnp.int32)
-    named = [destination[:, k] for k in range(top_count)]
-    dispatch = sum((place[:, None] == d[None, :]).astype(jnp.bfloat16) for d in named)
+    named = [destination[k] for k in range(top_count)]
     mixing = sum(
         jnp.where(d[:, None] == place[None, :], route_weights[:, k][:, None], 0.0)
         for k, d in enumerate(named)
@@ -124,8 +159,6 @@
     mixing_high = mixing.astype(jnp.bfloat16)
     mixing_low = (mixing - mixing_high.astype(jnp.float32)).astype(jnp.bfloat16)
 
-    mine = jnp.where(a == 0, tokens[:, :features], tokens[:, features:])
-    outgoing = jnp.dot(dispatch, mine, preferred_element_type=jnp.float32).astype(jnp.bfloat16)
     received = lax.all_to_all(
         outgoing.reshape(experts, capacity, features), "expert", split_axis=0, concat_axis=0, tiled=True
     )

time: 173 us -> 175 us (1.012)
  waiting for transfers between devices: 21.3 us -> 15.1 us
  starting transfers between devices: 28.6 us -> 32.4 us
  blocking collectives: 113 us -> 116 us
    all_to_all x1, blocking collectives: 23 us -> 27.5 us  [shards(): lax.all_to_all(mixed.reshape(sections, part, columns), 'section', split_a...]
    ppermute x5, starting transfers between devices: 25.1 us -> 28.9 us  [exchange(): lax.ppermute(value, axis, [(i, i ^ flip) for i in range(lax.axis_size(axi...]
    ppermute x5, waiting for transfers between devices: 13.2 us -> 9.65 us  [exchange(): lax.ppermute(value, axis, [(i, i ^ flip) for i in range(lax.axis_size(axi...]
    all_gather x1, blocking collectives: 41 us -> 37.9 us  [shards(): lax.all_gather(kept, 'section', axis=0, tiled=True)]
    all_to_all x1, waiting for transfers between devices: 8.07 us -> 5.4 us  [shards(): lax.all_to_all(outgoing.reshape(experts, capacity, features), 'expert', s...]
    all_to_all x1, blocking collectives: 24.9 us -> 26.7 us  [shards(): lax.all_to_all(partial_out.reshape(experts, capacity, columns), 'expert',...]
where the time goes in v5:
time: 175 us; the launch traced here: 174 us
  blocking collectives  116 us (66%)
  starting transfers between devices  32.4 us (19%)
  waiting for transfers between devices  15.1 us (9%)
  Pallas kernels  8.12 us (5%)
  local copies, waits for them, and re-layouts  2 us (1%)
    all_gather x1, blocking collectives, shards(): lax.all_gather(kept, 'section', axis=0, tiled=True)  37.9 us
    ppermute x5, starting transfers between devices, exchange(): lax.ppermute(value, axis, [(i, i ^ flip) for i in range(lax.axis_size(axi...  28.9 us
    all_to_all x1, blocking collectives, shards(): lax.all_to_all(mixed.reshape(sections, part, columns), 'section', split_a...  27.5 us
    all_to_all x1, blocking collectives, shards(): lax.all_to_all(partial_out.reshape(experts, capacity, columns), 'expert',...  26.7 us
    all_to_all x1, blocking collectives, shards(): lax.all_to_all(copies, 'section', split_axis=0, concat_axis=0, tiled=True)  24.3 us
    ppermute x5, waiting for transfers between devices, exchange(): lax.ppermute(value, axis, [(i, i ^ flip) for i in range(lax.axis_size(axi...  9.65 us
    all_to_all x1, waiting for transfers between devices, shards(): lax.all_to_all(outgoing.reshape(experts, capacity, features), 'expert', s...  5.4 us
    pallas_call x1, Pallas kernels, shards(): pl.pallas_call(front_kernel, out_shape=(shape, shape, jax.ShapeDtypeStruc...  4.11 us
  transfers between devices with their start and end apart: 6, of which 3 were waited for; matrix products, arithmetic and copies ran while one was open for 1% of the time, Pallas kernels for 0%

profile of v5, /device:TPU:6, one launch (start us, length us, event | category | flops | bytes accessed | tf_op | source)
XLA Modules:
  0.0 174.4 jit_solution(1570320959381992894)
XLA Ops:
  0.0 0.5 broadcast_in_dim.27.which_ref
  0.5 0.0 copy-start.2
  0.5 4.1 %shard_map.64 = (bf16[16,128,256]{2,1,0:T(8,128)(2,1)}, bf16[16,128,256]{2,1,0:T(8,128)(2,1)}, bf16[384,128]{1,0:T(8,128)(2,1)}, s32[2,128]{1,0:T(2,128)}) custom-call(s32[16]{0:T(128)} %broadcast_in_dim.27.which_ref, s32[2,128]{1,0:T(2,128)} %bitcast.35, bf16[128,256]{1,0:T(8,128)(2,1)} %tokens_ref.1, bf16[16,2,128,128]{3,2,1,0:T(8,128)(2,1)} %bitcast.30, ...), custom_call_target="tpu_custom_call" | custom-call | tf_op jit(solution)/shard_map/pallas_call | solution.py:126
  4.7 0.0 copy-start
  4.7 3.4 %collective-permute-start.2 = (bf16[2048,256]{1,0:T(8,128)(2,1)}, bf16[2048,256]{1,0:T(8,128)(2,1)S(1)}, u32[]{:S(2)}, u32[]{:S(2)}) collective-permute-start(bf16[2048,256]{1,0:T(8,128)(2,1)} %bitcast.36), channel_id=1, source_target_pairs={{0,2},{1,3},{2,0},{3,1},{4,6},{5,7},{6,4},{7,5},{8,10},{9,11},{10,... | collective-permute-start | bytes 3145736 | tf_op jit(solution)/shard_map/ppermute | solution.py:112
  8.1 14.5 %collective-permute-start = (bf16[2048,256]{1,0:T(8,128)(2,1)}, bf16[2048,256]{1,0:T(8,128)(2,1)S(1)}, u32[]{:S(2)}, u32[]{:S(2)}) collective-permute-start(bf16[2048,256]{1,0:T(8,128)(2,1)} %bitcast.37), channel_id=1, source_target_pairs={{0,1},{1,0},{2,3},{3,2},{4,5},{5,4},{6,7},{7,6},{8,9},{9,8},{10,11... | collective-permute-start | bytes 3145736 | tf_op jit(solution)/shard_map/ppermute | solution.py:112
  22.6 3.5 %all-to-all-start = ((bf16[16,24,128]{2,1,0:T(8,128)(2,1)}), bf16[16,24,128]{2,1,0:T(8,128)(2,1)S(1)}, u32[]{:S(2)}, u32[]{:S(2)}) async-start(bf16[16,24,128]{2,1,0:T(8,128)(2,1)} %bitcast.34), calls=%async_computation | async-start | bytes 196608 | tf_op jit(solution)/shard_map/all_to_all | solution.py:162
  26.1 1.9 %collective-permute-start.1 = (bf16[2048,256]{1,0:T(8,128)(2,1)}, bf16[2048,256]{1,0:T(8,128)(2,1)}, u32[]{:S(2)}, u32[]{:S(2)}) collective-permute-start(bf16[2048,256]{1,0:T(8,128)(2,1)} %bitcast.26), channel_id=1, source_target_pairs={{0,3},{1,2},{2,1},{3,0},{4,7},{5,6},{6,5},{7,4},{8,11},{9,10},{10,... | collective-permute-start | bytes 3145736 | tf_op jit(solution)/shard_map/ppermute | solution.py:112
  28.1 0.0 copy-done.2
  28.1 0.7 slice_bitcast_fusion.3
  28.8 0.1 subtract_convert_fusion
  29.0 5.4 %all-to-all-done = bf16[16,24,128]{2,1,0:T(8,128)(2,1)S(1)} async-done(((bf16[16,24,128]{2,1,0:T(8,128)(2,1)}), bf16[16,24,128]{2,1,0:T(8,128)(2,1)S(1)}, u32[]{:S(2)}, u32[]{:S(2)}) %all-to-all-start) | async-done | bytes 98336 | tf_op jit(solution)/shard_map/all_to_all | solution.py:162
  34.4 37.9 %all_gather.3 = bf16[3072,128]{1,0:T(8,128)(2,1)S(1)} all-gather(bf16[192,128]{1,0:T(8,128)(2,1)S(1)} %constant_dynamic-slice_fusion), channel_id=1, replica_groups=mesh['section'=16,'expert'=16,'seq'=4] {'section'}, dimensions={0}, use_global_device_ids=true | all-gather | bytes 835584 | tf_op jit(solution)/shard_map/all_gather | solution.py:168
  72.3 0.0 collective-permute-done.1.w2_ref
  72.3 0.0 collective-permute-done.2.w3_ref
  72.3 0.0 collective-permute-done.w1_ref
  72.3 0.0 copy-done
  72.4 2.2 %shard_map.65 = (f32[4,192,256]{2,1,0:T(8,128)S(1)}, bf16[4,192,256]{2,1,0:T(8,128)(2,1)S(1)}) custom-call(bf16[16,192,128]{2,1,0:T(8,128)(2,1)S(1)} %bitcast.23, bf16[2048,256]{1,0:T(8,128)(2,1)S(1)} %bitcast.27, bf16[2048,256]{1,0:T(8,128)(2,1)S(1)} %collective-permute-done.w1_ref, bf16[2048,256]{1,0:T(8,128)(2,1)} %collective-permute-done.1.w2_ref, ...), custom_call_target="tpu_custom_call" | custom-call | tf_op jit(solution)/shard_map/pallas_call | solution.py:170
  74.6 0.0 copy-start.1
  74.6 4.3 %collective-permute-start.3 = (bf16[4,192,256]{2,1,0:T(8,128)(2,1)S(1)}, bf16[4,192,256]{2,1,0:T(8,128)(2,1)S(1)}, u32[]{:S(2)}, u32[]{:S(2)}) collective-permute-start(bf16[4,192,256]{2,1,0:T(8,128)(2,1)S(1)} %get-tuple-element.20), channel_id=1, source_target_pairs={{0,1},{1,0},{2,3},{3,2},{4,5},{5,4},{6,7},{7,6},{8,9},{9,8},{10,11... | collective-permute-start | bytes 1179656 | tf_op jit(solution)/shard_map/ppermute | solution.py:112
  78.8 5.7 %collective-permute-done.3.got_ref = bf16[4,192,256]{2,1,0:T(8,128)(2,1)S(1)} collective-permute-done((bf16[4,192,256]{2,1,0:T(8,128)(2,1)S(1)}, bf16[4,192,256]{2,1,0:T(8,128)(2,1)S(1)}, u32[]{:S(2)}, u32[]{:S(2)}) %collective-permute-start.3) | collective-permute-done | bytes 393248 | tf_op jit(solution)/shard_map/ppermute | solution.py:112
  84.6 0.2 shard_map.66.own_ref
  84.7 4.8 %collective-permute-start.4 = (bf16[4,192,128]{2,1,0:T(8,128)(2,1)S(1)}, bf16[4,192,128]{2,1,0:T(8,128)(2,1)S(1)}, u32[]{:S(2)}, u32[]{:S(2)}) collective-permute-start(bf16[4,192,128]{2,1,0:T(8,128)(2,1)S(1)} %shard_map.66.own_ref), channel_id=1, source_target_pairs={{0,3},{1,2},{2,1},{3,0},{4,7},{5,6},{6,5},{7,4},{8,11},{9,10},{10,... | collective-permute-start | bytes 589832 | tf_op jit(solution)/shard_map/ppermute | solution.py:112
  89.5 0.1 pad_add_fusion.place_ref
  89.6 3.9 %collective-permute-done.4.got_ref = bf16[4,192,128]{2,1,0:T(8,128)(2,1)S(1)} collective-permute-done((bf16[4,192,128]{2,1,0:T(8,128)(2,1)S(1)}, bf16[4,192,128]{2,1,0:T(8,128)(2,1)S(1)}, u32[]{:S(2)}, u32[]{:S(2)}) %collective-permute-start.4) | collective-permute-done | bytes 196640 | tf_op jit(solution)/shard_map/ppermute | solution.py:112
  93.5 0.0 copy-done.1
  93.5 1.2 shard_map.67
  94.7 26.7 %all_to_all.20 = bf16[16,24,1024]{2,1,0:T(8,128)(2,1)S(1)} all-to-all(bf16[16,24,1024]{2,1,0:T(8,128)(2,1)S(1)} %bitcast.24), channel_id=1, replica_groups=mesh['section'=16,'expert'=16,'seq'=4] {'expert'}, dimensions={0} | all-to-all | bytes 1572864 | tf_op jit(solution)/shard_map/all_to_all | solution.py:198
  121.4 0.4 shard_map.68
  121.8 27.5 %all_to_all.21.terms_ref = bf16[16,8,1024]{2,1,0:T(8,128)(2,1)S(1)} all-to-all(bf16[16,8,1024]{2,1,0:T(8,128)(2,1)S(1)} %bitcast.29), channel_id=1, replica_groups=mesh['section'=16,'expert'=16,'seq'=4] {'section'}, dimensions={0} | all-to-all | bytes 524288 | tf_op jit(solution)/shard_map/all_to_all | solution.py:209
  149.4 24.3 %all_to_all.22 = bf16[16,8,1024]{2,1,0:T(8,128)(2,1)S(1)} all-to-all(bf16[16,8,1024]{2,1,0:T(8,128)(2,1)S(1)} %shard_map.69), channel_id=1, replica_groups=mesh['section'=16,'expert'=16,'seq'=4] {'section'}, dimensions={0} | all-to-all | bytes 524288 | tf_op jit(solution)/shard_map/all_to_all | solution.py:219
  173.7 0.7 copy.8
  (3 shorter events, 0.1 us)
Async XLA Ops:
  0.5 27.5 %copy-start.2 = (f32[128,2]{0,1:T(2,128)S(1)}, f32[128,2]{0,1:T(2,128)}, u32[]{:S(2)}) copy-start(f32[128,2]{0,1:T(2,128)} %param.8) | copy-start | bytes 3076
  4.7 67.7 %copy-start = (bf16[16,128,256]{2,1,0:T(8,128)(2,1)S(1)}, bf16[16,128,256]{2,1,0:T(8,128)(2,1)}, u32[]{:S(2)}) copy-start(bf16[16,128,256]{2,1,0:T(8,128)(2,1)} %get-tuple-element.17) | copy-start | bytes 3145732
  4.7 67.7 %collective-permute-start.2 = (bf16[2048,256]{1,0:T(8,128)(2,1)}, bf16[2048,256]{1,0:T(8,128)(2,1)S(1)}, u32[]{:S(2)}, u32[]{:S(2)}) collective-permute-start(bf16[2048,256]{1,0:T(8,128)(2,1)} %bitcast.36), channel_id=1, source_target_pairs={{0,2},{1,3},{2,0},{3,1},{4,6},{5,7},{6,4},{7,5},{8,10},{9,11},{10,... | collective-permute-start | bytes 3145736 | tf_op jit(solution)/shard_map/ppermute | solution.py:112
  8.1 64.2 %collective-permute-start = (bf16[2048,256]{1,0:T(8,128)(2,1)}, bf16[2048,256]{1,0:T(8,128)(2,1)S(1)}, u32[]{:S(2)}, u32[]{:S(2)}) collective-permute-start(bf16[2048,256]{1,0:T(8,128)(2,1)} %bitcast.37), channel_id=1, source_target_pairs={{0,1},{1,0},{2,3},{3,2},{4,5},{5,4},{6,7},{7,6},{8,9},{9,8},{10,11... | collective-permute-start | bytes 3145736 | tf_op jit(solution)/shard_map/ppermute | solution.py:112
  22.6 11.8 %all-to-all-start = ((bf16[16,24,128]{2,1,0:T(8,128)(2,1)}), bf16[16,24,128]{2,1,0:T(8,128)(2,1)S(1)}, u32[]{:S(2)}, u32[]{:S(2)}) async-start(bf16[16,24,128]{2,1,0:T(8,128)(2,1)} %bitcast.34), calls=%async_computation | async-start | bytes 196608 | tf_op jit(solution)/shard_map/all_to_all | solution.py:162
  26.1 46.2 %collective-permute-start.1 = (bf16[2048,256]{1,0:T(8,128)(2,1)}, bf16[2048,256]{1,0:T(8,128)(2,1)}, u32[]{:S(2)}, u32[]{:S(2)}) collective-permute-start(bf16[2048,256]{1,0:T(8,128)(2,1)} %bitcast.26), channel_id=1, source_target_pairs={{0,3},{1,2},{2,1},{3,0},{4,7},{5,6},{6,5},{7,4},{8,11},{9,10},{10,... | collective-permute-start | bytes 3145736 | tf_op jit(solution)/shard_map/ppermute | solution.py:112
  74.6 19.0 %copy-start.1 = (bf16[1,512,1024]{2,1,0:T(8,128)(2,1)S(1)}, bf16[1,512,1024]{2,1,0:T(8,128)(2,1)}, u32[]{:S(2)}) copy-start(bf16[1,512,1024]{2,1,0:T(8,128)(2,1)} %param.11) | copy-start | bytes 3145732
  74.6 10.0 %collective-permute-start.3 = (bf16[4,192,256]{2,1,0:T(8,128)(2,1)S(1)}, bf16[4,192,256]{2,1,0:T(8,128)(2,1)S(1)}, u32[]{:S(2)}, u32[]{:S(2)}) collective-permute-start(bf16[4,192,256]{2,1,0:T(8,128)(2,1)S(1)} %get-tuple-element.20), channel_id=1, source_target_pairs={{0,1},{1,0},{2,3},{3,2},{4,5},{5,4},{6,7},{7,6},{8,9},{9,8},{10,11... | collective-permute-start | bytes 1179656 | tf_op jit(solution)/shard_map/ppermute | solution.py:112
  84.7 8.8 %collective-permute-start.4 = (bf16[4,192,128]{2,1,0:T(8,128)(2,1)S(1)}, bf16[4,192,128]{2,1,0:T(8,128)(2,1)S(1)}, u32[]{:S(2)}, u32[]{:S(2)}) collective-permute-start(bf16[4,192,128]{2,1,0:T(8,128)(2,1)S(1)} %shard_map.66.own_ref), channel_id=1, source_target_pairs={{0,3},{1,2},{2,1},{3,0},{4,7},{5,6},{6,5},{7,4},{8,11},{9,10},{10,... | collective-permute-start | bytes 589832 | tf_op jit(solution)/shard_map/ppermute | solution.py:112

commit v6 on v4

--- a/solution.py
+++ b/solution.py
@@ -1,3 +1,5 @@
+import functools
+
 import jax
 import jax.numpy as jnp
 from jax import lax
@@ -12,19 +14,40 @@
 
 
 def split_kernel(which_ref, gate_ref, up_ref, same_ref, other_ref, sems):
-    units = gate_ref.shape[3]
-    copies = []
-    for out_ref, turn in ((other_ref, 1), (same_ref, 0)):
-        for k, ref in enumerate((gate_ref, up_ref)):
-            copies.append(
-                pltpu.make_async_copy(
-                    ref.at[:, which_ref[0] ^ turn], out_ref.at[:, :, k * units : (k + 1) * units], sems.at[2 * turn + k]
-                )
-            )
+    copies = [
+        pltpu.make_async_copy(ref.at[:, which_ref[0] ^ turn], out_ref.at[k], sems.at[2 * turn + k])
+        for out_ref, turn in ((other_ref, 1), (same_ref, 0))
+        for k, ref in enumerate((gate_ref, up_ref))
+    ]
     for copy in copies:
         copy.start()
     for copy in copies:
         copy.wait()
+
+
+def route_kernel(experts, which_ref, ids_ref, tokens_ref, rows_ref, place_ref):
+    top_count, count = ids_ref.shape
+    rows_total = rows_ref.shape[0]
+    capacity = rows_total // experts
+    features = tokens_ref.shape[1] // 2
+    expert = lax.broadcasted_iota(jnp.int32, (experts, count), 0)
+    ids = [ids_ref[k : k + 1, :] for k in range(top_count)]
+    named = [jnp.where(expert == i, 1.0, 0.0) for i in ids]
+    before = lax.broadcasted_iota(jnp.int32, (count, count), 0) < lax.broadcasted_iota(jnp.int32, (count, count), 1)
+    earlier = jnp.dot(
+        sum(named).astype(jnp.bfloat16),
+        jnp.where(before, 1.0, 0.0).astype(jnp.bfloat16),
+        preferred_element_type=jnp.float32,
+    )
+    row = lax.broadcasted_iota(jnp.int32, (rows_total, count), 0)
+    dispatch = jnp.zeros((rows_total, count), jnp.float32)
+    for k in range(top_count):
+        slot = jnp.sum(named[k] * earlier, axis=0, keepdims=True).astype(jnp.int32)
+        place = ids[k] * capacity + slot
+        place_ref[k : k + 1, :] = place
+        dispatch = dispatch + jnp.where(row == place, 1.0, 0.0)
+    mine = tokens_ref[:, pl.ds(pl.multiple_of(which_ref[0] * features, features), features)]
+    rows_ref[...] = jnp.dot(dispatch.astype(jnp.bfloat16), mine, preferred_element_type=jnp.float32).astype(jnp.bfloat16)
 
 
 def up_kernel(x_ref, w0_ref, w1_ref, w2_ref, w3_ref, own_ref, send_ref):
@@ -33,7 +56,9 @@
         total = None
         for s in range(0, sections, 2):
             rows = jnp.concatenate([x_ref[s], x_ref[s + 1]], axis=1)
-            term = jnp.dot(rows, w_ref[s * width : (s + 2) * width, :], preferred_element_type=jnp.float32)
+            depth = slice(s * width, (s + 2) * width)
+            both = jnp.concatenate([w_ref[0, depth, :], w_ref[1, depth, :]], axis=1)
+            term = jnp.dot(rows, both, preferred_element_type=jnp.float32)
             total = term if total is None else total + term
         own_ref[block] = total
         send_ref[block] = total.astype(jnp.bfloat16)
@@ -89,7 +114,8 @@
     q = lax.axis_index("seq")
     a, b = (q ^ (q >> 1)) & 1, q >> 1
 
-    shape = jax.ShapeDtypeStruct((sections, features, 2 * units), jnp.bfloat16)
+    which = a.astype(jnp.int32).reshape(1)
+    shape = jax.ShapeDtypeStruct((2, sections, features, units), jnp.bfloat16)
     same, other = pl.pallas_call(
         split_kernel,
         out_shape=(shape, shape),
@@ -97,26 +123,27 @@
         out_specs=(VMEM, VMEM),
         scratch_shapes=[pltpu.SemaphoreType.DMA((4,))],
     )(
-        a.astype(jnp.int32).reshape(1),
+        which,
         gate_weight[0].reshape(sections, 2, features, units),
         up_weight[0].reshape(sections, 2, features, units),
     )
-    same, other = (w.reshape(sections * features, 2 * units) for w in (same, other))
+    same, other = (w.reshape(2, sections * features, units) for w in (same, other))
     w1 = exchange(other, "seq", 1)
     w2 = exchange(same, "seq", 3)
     w3 = exchange(other, "seq", 2)
 
-    flat_ids = route_ids.reshape(-1)
-    pairs = tok_rows * top_count
-    onehot = flat_ids[:, None] == jnp.arange(experts, dtype=jnp.int32)[None, :]
-    order = jnp.arange(pairs, dtype=jnp.int32)
-    below = (order[:, None] > order[None, :]).astype(jnp.bfloat16)
-    earlier = jnp.dot(below, onehot.astype(jnp.bfloat16), preferred_element_type=jnp.float32)
-    slot_index = jnp.sum(jnp.where(onehot, earlier, 0.0), axis=1).astype(jnp.int32)
-    destination = (flat_ids * capacity + slot_index).reshape(tok_rows, top_count)
+    outgoing, destination = pl.pallas_call(
+        functools.partial(route_kernel, experts),
+        out_shape=(
+            jax.ShapeDtypeStruct((rows_total, features), jnp.bfloat16),
+            jax.ShapeDtypeStruct((top_count, tok_rows), jnp.int32),
+        ),
+        in_specs=[SMEM, VMEM, VMEM],
+        out_specs=(VMEM, VMEM),
+        compiler_params=PARAMS,
+    )(which, route_ids.T, tokens)
     place = jnp.arange(rows_total, dtype=jnp.int32)
-    named = [destination[:, k] for k in range(top_count)]
-    dispatch = sum((place[:, None] == d[None, :]).astype(jnp.bfloat16) for d in named)
+    named = [destination[k] for k in range(top_count)]
     mixing = sum(
         jnp.where(d[:, None] == place[None, :], route_weights[:, k][:, None], 0.0)
         for k, d in enumerate(named)
@@ -124,8 +151,6 @@
     mixing_high = mixing.astype(jnp.bfloat16)
     mixing_low = (mixing - mixing_high.astype(jnp.float32)).astype(jnp.bfloat16)
 
-    mine = jnp.where(a == 0, tokens[:, :features], tokens[:, features:])
-    outgoing = jnp.dot(dispatch, mine, preferred_element_type=jnp.float32).astype(jnp.bfloat16)
     received = lax.all_to_all(
         outgoing.reshape(experts, capacity, features), "expert", split_axis=0, concat_axis=0, tiled=True
     )

time: 173 us -> 173 us (level)
  waiting for transfers between devices: 21.3 us -> 15.9 us
  starting transfers between devices: 28.6 us -> 32.4 us
  blocking collectives: 113 us -> 115 us
    all_to_all x1, blocking collectives: 23 us -> 27.3 us  [shards(): lax.all_to_all(mixed.reshape(sections, part, columns), 'section', split_a...]
    ppermute x5, starting transfers between devices: 25.1 us -> 28.9 us  [exchange(): lax.ppermute(value, axis, [(i, i ^ flip) for i in range(lax.axis_size(axi...]
    ppermute x5, waiting for transfers between devices: 13.2 us -> 9.79 us  [exchange(): lax.ppermute(value, axis, [(i, i ^ flip) for i in range(lax.axis_size(axi...]
    all_gather x1, blocking collectives: 41 us -> 38 us  [shards(): lax.all_gather(kept, 'section', axis=0, tiled=True)]
    all_to_all x1, waiting for transfers between devices: 8.07 us -> 6.13 us  [shards(): lax.all_to_all(outgoing.reshape(experts, capacity, features), 'expert', s...]
  transfers between devices with their start and end apart: 6 -> 6, of which waited for: 3 -> 3; matrix products, arithmetic and copies ran while one was open for 1% -> 0% of each run, Pallas kernels for 0% -> 1%
where the time goes in v6:
time: 173 us
  blocking collectives  115 us (66%)
  starting transfers between devices  32.4 us (19%)
  waiting for transfers between devices  15.9 us (9%)
  Pallas kernels  7.9 us (5%)
    all_gather x1, blocking collectives, shards(): lax.all_gather(kept, 'section', axis=0, tiled=True)  38 us
    ppermute x5, starting transfers between devices, exchange(): lax.ppermute(value, axis, [(i, i ^ flip) for i in range(lax.axis_size(axi...  28.9 us
    all_to_all x1, blocking collectives, shards(): lax.all_to_all(mixed.reshape(sections, part, columns), 'section', split_a...  27.3 us
    all_to_all x1, blocking collectives, shards(): lax.all_to_all(partial_out.reshape(experts, capacity, columns), 'expert',...  25.8 us
    all_to_all x1, blocking collectives, shards(): lax.all_to_all(copies, 'section', split_axis=0, concat_axis=0, tiled=True)  24.4 us
    ppermute x5, waiting for transfers between devices, exchange(): lax.ppermute(value, axis, [(i, i ^ flip) for i in range(lax.axis_size(axi...  9.79 us
    all_to_all x1, waiting for transfers between devices, shards(): lax.all_to_all(outgoing.reshape(experts, capacity, features), 'expert', s...  6.13 us
    all_to_all x1, starting transfers between devices, shards(): lax.all_to_all(outgoing.reshape(experts, capacity, features), 'expert', s...  3.51 us
  transfers between devices with their start and end apart: 6, of which 3 were waited for; matrix products, arithmetic and copies ran while one was open for 0% of the time, Pallas kernels for 1%

profile of v6, /device:TPU:6, one launch (start us, length us, event | category | flops | bytes accessed | tf_op | source)
XLA Modules:
  0.0 172.7 jit_solution(4065244676970006399)
XLA Ops:
  0.0 0.0 copy-start.2
  0.0 0.0 copy-start.3
  0.0 0.0 copy-start.4
  0.0 2.9 %shard_map.65 = (bf16[2,16,128,128]{3,2,1,0:T(8,128)(2,1)}, bf16[2,16,128,128]{3,2,1,0:T(8,128)(2,1)}) custom-call(s32[1]{0:T(128)} %bitcast.2.which_ref, bf16[16,2,128,128]{3,2,1,0:T(8,128)(2,1)} %bitcast.32, bf16[16,2,128,128]{3,2,1,0:T(8,128)(2,1)} %bitcast.33), custom_call_target="tpu_custom_call" | custom-call | tf_op jit(solution)/shard_map/pallas_call | solution.py:119
  3.0 0.0 copy-start
  3.0 3.4 %collective-permute-start.2 = (bf16[2,2048,128]{2,1,0:T(8,128)(2,1)}, bf16[2,2048,128]{2,1,0:T(8,128)(2,1)S(1)}, u32[]{:S(2)}, u32[]{:S(2)}) collective-permute-start(bf16[2,2048,128]{2,1,0:T(8,128)(2,1)} %bitcast.36), channel_id=1, source_target_pairs={{0,2},{1,3},{2,0},{3,1},{4,6},{5,7},{6,4},{7,5},{8,10},{9,11},{10,... | collective-permute-start | bytes 3145736 | tf_op jit(solution)/shard_map/ppermute | solution.py:104
  6.4 14.5 %collective-permute-start = (bf16[2,2048,128]{2,1,0:T(8,128)(2,1)}, bf16[2,2048,128]{2,1,0:T(8,128)(2,1)S(1)}, u32[]{:S(2)}, u32[]{:S(2)}) collective-permute-start(bf16[2,2048,128]{2,1,0:T(8,128)(2,1)} %bitcast.37), channel_id=1, source_target_pairs={{0,1},{1,0},{2,3},{3,2},{4,5},{5,4},{6,7},{7,6},{8,9},{9,8},{10,11... | collective-permute-start | bytes 3145736 | tf_op jit(solution)/shard_map/ppermute | solution.py:104
  20.9 0.0 copy-done.2
  20.9 0.0 copy-done.3
  20.9 1.0 shard_map.64
  21.9 3.5 %all-to-all-start = ((bf16[16,24,128]{2,1,0:T(8,128)(2,1)}), bf16[16,24,128]{2,1,0:T(8,128)(2,1)S(1)}, u32[]{:S(2)}, u32[]{:S(2)}) async-start(bf16[16,24,128]{2,1,0:T(8,128)(2,1)} %bitcast.4), calls=%async_computation | async-start | bytes 196608 | tf_op jit(solution)/shard_map/all_to_all | solution.py:154
  25.4 1.9 %collective-permute-start.1 = (bf16[2,2048,128]{2,1,0:T(8,128)(2,1)}, bf16[2,2048,128]{2,1,0:T(8,128)(2,1)}, u32[]{:S(2)}, u32[]{:S(2)}) collective-permute-start(bf16[2,2048,128]{2,1,0:T(8,128)(2,1)} %bitcast.27), channel_id=1, source_target_pairs={{0,3},{1,2},{2,1},{3,0},{4,7},{5,6},{6,5},{7,4},{8,11},{9,10},{10,... | collective-permute-start | bytes 3145736 | tf_op jit(solution)/shard_map/ppermute | solution.py:104
  27.3 0.0 copy-done.4
  27.4 0.1 subtract_convert_fusion
  27.5 6.1 %all-to-all-done = bf16[16,24,128]{2,1,0:T(8,128)(2,1)S(1)} async-done(((bf16[16,24,128]{2,1,0:T(8,128)(2,1)}), bf16[16,24,128]{2,1,0:T(8,128)(2,1)S(1)}, u32[]{:S(2)}, u32[]{:S(2)}) %all-to-all-start) | async-done | bytes 98336 | tf_op jit(solution)/shard_map/all_to_all | solution.py:154
  33.6 38.0 %all_gather.3 = bf16[3072,128]{1,0:T(8,128)(2,1)S(1)} all-gather(bf16[192,128]{1,0:T(8,128)(2,1)S(1)} %constant_dynamic-slice_fusion), channel_id=1, replica_groups=mesh['section'=16,'expert'=16,'seq'=4] {'section'}, dimensions={0}, use_global_device_ids=true | all-gather | bytes 835584 | tf_op jit(solution)/shard_map/all_gather | solution.py:160
  71.6 0.0 collective-permute-done.2.w3_ref
  71.6 0.0 collective-permute-done.w1_ref
  71.6 0.0 collective-permute-done.1.w2_ref
  71.6 0.0 copy-done
  71.6 2.2 %shard_map.66 = (f32[4,192,256]{2,1,0:T(8,128)S(1)}, bf16[4,192,256]{2,1,0:T(8,128)(2,1)S(1)}) custom-call(bf16[16,192,128]{2,1,0:T(8,128)(2,1)S(1)} %bitcast.24, bf16[2,2048,128]{2,1,0:T(8,128)(2,1)S(1)} %bitcast.28, bf16[2,2048,128]{2,1,0:T(8,128)(2,1)S(1)} %collective-permute-done.w1_ref, bf16[2,2048,128]{2,1,0:T(8,128)(2,1)} %collective-permute-done.1.w2_ref, ...), custom_call_target="tpu_custom_call" | custom-call | tf_op jit(solution)/shard_map/pallas_call | solution.py:162
  73.8 0.0 copy-start.1
  73.8 4.4 %collective-permute-start.3 = (bf16[4,192,256]{2,1,0:T(8,128)(2,1)S(1)}, bf16[4,192,256]{2,1,0:T(8,128)(2,1)S(1)}, u32[]{:S(2)}, u32[]{:S(2)}) collective-permute-start(bf16[4,192,256]{2,1,0:T(8,128)(2,1)S(1)} %get-tuple-element.20), channel_id=1, source_target_pairs={{0,1},{1,0},{2,3},{3,2},{4,5},{5,4},{6,7},{7,6},{8,9},{9,8},{10,11... | collective-permute-start | bytes 1179656 | tf_op jit(solution)/shard_map/ppermute | solution.py:104
  78.2 5.7 %collective-permute-done.3.got_ref = bf16[4,192,256]{2,1,0:T(8,128)(2,1)S(1)} collective-permute-done((bf16[4,192,256]{2,1,0:T(8,128)(2,1)S(1)}, bf16[4,192,256]{2,1,0:T(8,128)(2,1)S(1)}, u32[]{:S(2)}, u32[]{:S(2)}) %collective-permute-start.3) | collective-permute-done | bytes 393248 | tf_op jit(solution)/shard_map/ppermute | solution.py:104
  84.0 0.2 shard_map.67.own_ref
  84.1 4.6 %collective-permute-start.4 = (bf16[4,192,128]{2,1,0:T(8,128)(2,1)S(1)}, bf16[4,192,128]{2,1,0:T(8,128)(2,1)S(1)}, u32[]{:S(2)}, u32[]{:S(2)}) collective-permute-start(bf16[4,192,128]{2,1,0:T(8,128)(2,1)S(1)} %shard_map.67.own_ref), channel_id=1, source_target_pairs={{0,3},{1,2},{2,1},{3,0},{4,7},{5,6},{6,5},{7,4},{8,11},{9,10},{10,... | collective-permute-start | bytes 589832 | tf_op jit(solution)/shard_map/ppermute | solution.py:104
  88.8 0.1 pad_add_fusion.place_ref
  88.9 4.0 %collective-permute-done.4.got_ref = bf16[4,192,128]{2,1,0:T(8,128)(2,1)S(1)} collective-permute-done((bf16[4,192,128]{2,1,0:T(8,128)(2,1)S(1)}, bf16[4,192,128]{2,1,0:T(8,128)(2,1)S(1)}, u32[]{:S(2)}, u32[]{:S(2)}) %collective-permute-start.4) | collective-permute-done | bytes 196640 | tf_op jit(solution)/shard_map/ppermute | solution.py:104
  92.9 0.0 copy-done.1
  92.9 1.2 shard_map.68
  94.1 25.8 %all_to_all.20 = bf16[16,24,1024]{2,1,0:T(8,128)(2,1)S(1)} all-to-all(bf16[16,24,1024]{2,1,0:T(8,128)(2,1)S(1)} %bitcast.25), channel_id=1, replica_groups=mesh['section'=16,'expert'=16,'seq'=4] {'expert'}, dimensions={0} | all-to-all | bytes 1572864 | tf_op jit(solution)/shard_map/all_to_all | solution.py:190
  119.9 0.4 shard_map.69
  120.4 27.3 %all_to_all.21.terms_ref = bf16[16,8,1024]{2,1,0:T(8,128)(2,1)S(1)} all-to-all(bf16[16,8,1024]{2,1,0:T(8,128)(2,1)S(1)} %bitcast.30), channel_id=1, replica_groups=mesh['section'=16,'expert'=16,'seq'=4] {'section'}, dimensions={0} | all-to-all | bytes 524288 | tf_op jit(solution)/shard_map/all_to_all | solution.py:201
  147.7 24.4 %all_to_all.22 = bf16[16,8,1024]{2,1,0:T(8,128)(2,1)S(1)} all-to-all(bf16[16,8,1024]{2,1,0:T(8,128)(2,1)S(1)} %shard_map.70), channel_id=1, replica_groups=mesh['section'=16,'expert'=16,'seq'=4] {'section'}, dimensions={0} | all-to-all | bytes 524288 | tf_op jit(solution)/shard_map/all_to_all | solution.py:211
  172.0 0.7 copy.8
  (4 shorter events, 0.1 us)
Async XLA Ops:
  0.0 20.9 %copy-start.2 = (bf16[128,256]{1,0:T(8,128)(2,1)S(1)}, bf16[128,256]{1,0:T(8,128)(2,1)}, u32[]{:S(2)}) copy-start(bf16[128,256]{1,0:T(8,128)(2,1)} %tokens_ref.1) | copy-start | bytes 196612
  0.0 20.9 %copy-start.3 = (s32[128,2]{0,1:T(2,128)S(1)}, s32[128,2]{0,1:T(2,128)}, u32[]{:S(2)}) copy-start(s32[128,2]{0,1:T(2,128)} %param.7) | copy-start | bytes 3076
  0.0 27.3 %copy-start.4 = (f32[128,2]{0,1:T(2,128)S(1)}, f32[128,2]{0,1:T(2,128)}, u32[]{:S(2)}) copy-start(f32[128,2]{0,1:T(2,128)} %param.8) | copy-start | bytes 3076
  3.0 68.6 %copy-start = (bf16[2,16,128,128]{3,2,1,0:T(8,128)(2,1)S(1)}, bf16[2,16,128,128]{3,2,1,0:T(8,128)(2,1)}, u32[]{:S(2)}) copy-start(bf16[2,16,128,128]{3,2,1,0:T(8,128)(2,1)} %get-tuple-element.17) | copy-start | bytes 3145732
  3.0 68.6 %collective-permute-start.2 = (bf16[2,2048,128]{2,1,0:T(8,128)(2,1)}, bf16[2,2048,128]{2,1,0:T(8,128)(2,1)S(1)}, u32[]{:S(2)}, u32[]{:S(2)}) collective-permute-start(bf16[2,2048,128]{2,1,0:T(8,128)(2,1)} %bitcast.36), channel_id=1, source_target_pairs={{0,2},{1,3},{2,0},{3,1},{4,6},{5,7},{6,4},{7,5},{8,10},{9,11},{10,... | collective-permute-start | bytes 3145736 | tf_op jit(solution)/shard_map/ppermute | solution.py:104
  6.4 65.2 %collective-permute-start = (bf16[2,2048,128]{2,1,0:T(8,128)(2,1)}, bf16[2,2048,128]{2,1,0:T(8,128)(2,1)S(1)}, u32[]{:S(2)}, u32[]{:S(2)}) collective-permute-start(bf16[2,2048,128]{2,1,0:T(8,128)(2,1)} %bitcast.37), channel_id=1, source_target_pairs={{0,1},{1,0},{2,3},{3,2},{4,5},{5,4},{6,7},{7,6},{8,9},{9,8},{10,11... | collective-permute-start | bytes 3145736 | tf_op jit(solution)/shard_map/ppermute | solution.py:104
  21.9 11.8 %all-to-all-start = ((bf16[16,24,128]{2,1,0:T(8,128)(2,1)}), bf16[16,24,128]{2,1,0:T(8,128)(2,1)S(1)}, u32[]{:S(2)}, u32[]{:S(2)}) async-start(bf16[16,24,128]{2,1,0:T(8,128)(2,1)} %bitcast.4), calls=%async_computation | async-start | bytes 196608 | tf_op jit(solution)/shard_map/all_to_all | solution.py:154
  25.4 46.2 %collective-permute-start.1 = (bf16[2,2048,128]{2,1,0:T(8,128)(2,1)}, bf16[2,2048,128]{2,1,0:T(8,128)(2,1)}, u32[]{:S(2)}, u32[]{:S(2)}) collective-permute-start(bf16[2,2048,128]{2,1,0:T(8,128)(2,1)} %bitcast.27), channel_id=1, source_target_pairs={{0,3},{1,2},{2,1},{3,0},{4,7},{5,6},{6,5},{7,4},{8,11},{9,10},{10,... | collective-permute-start | bytes 3145736 | tf_op jit(solution)/shard_map/ppermute | solution.py:104
  73.8 19.1 %copy-start.1 = (bf16[1,512,1024]{2,1,0:T(8,128)(2,1)S(1)}, bf16[1,512,1024]{2,1,0:T(8,128)(2,1)}, u32[]{:S(2)}) copy-start(bf16[1,512,1024]{2,1,0:T(8,128)(2,1)} %param.11) | copy-start | bytes 3145732
  73.8 10.1 %collective-permute-start.3 = (bf16[4,192,256]{2,1,0:T(8,128)(2,1)S(1)}, bf16[4,192,256]{2,1,0:T(8,128)(2,1)S(1)}, u32[]{:S(2)}, u32[]{:S(2)}) collective-permute-start(bf16[4,192,256]{2,1,0:T(8,128)(2,1)S(1)} %get-tuple-element.20), channel_id=1, source_target_pairs={{0,1},{1,0},{2,3},{3,2},{4,5},{5,4},{6,7},{7,6},{8,9},{9,8},{10,11... | collective-permute-start | bytes 1179656 | tf_op jit(solution)/shard_map/ppermute | solution.py:104
  84.1 8.8 %collective-permute-start.4 = (bf16[4,192,128]{2,1,0:T(8,128)(2,1)S(1)}, bf16[4,192,128]{2,1,0:T(8,128)(2,1)S(1)}, u32[]{:S(2)}, u32[]{:S(2)}) collective-permute-start(bf16[4,192,128]{2,1,0:T(8,128)(2,1)S(1)} %shard_map.67.own_ref), channel_id=1, source_target_pairs={{0,3},{1,2},{2,1},{3,0},{4,7},{5,6},{6,5},{7,4},{8,11},{9,10},{10,... | collective-permute-start | bytes 589832 | tf_op jit(solution)/shard_map/ppermute | solution.py:104
